TPU v7x, 32 devices: a whole 2x2x4 slice. The times are simulated.
32 devices in a mesh: blk: 16 (over z, y, x), dp: 2 (over core).
Axes of the slice: x: 2, y: 2, z: 4, core: 2. Of those that a mesh axis runs over, the one named last changes fastest.
Arguments:
- tokens: bfloat16 [7168, 2048], P('blk', 'dp'), may hold values from -6 to 6
- cotangent: bfloat16 [7168, 2048], P('blk', 'dp'), may hold values from -6 to 6
- block_tokens: int32 [224, 64], P('blk'), may hold values from 0 to 447, as said below
- block_expert: int32 [224], P('blk'), may hold values from -1 to 15, as said below
- block_gate: bfloat16 [224, 64], P('blk'), may hold values from 0.099609375 to 1
- w_gate: bfloat16 [16, 2048, 768], P('blk', None, 'dp'), may hold values from -0.125 to 0.125
- w_up: bfloat16 [16, 2048, 768], P('blk', None, 'dp'), may hold values from -0.125 to 0.125
- w_down: bfloat16 [16, 768, 2048], P('blk', 'dp'), may hold values from -0.21875 to 0.21875
Outputs:
- mixed: bfloat16 [7168, 2048], P('blk', 'dp')
- grad_tokens: bfloat16 [7168, 2048], P('blk', 'dp')
- grad_gate: bfloat16 [16, 2048, 768], P('blk', None, 'dp')
- grad_up: bfloat16 [16, 2048, 768], P('blk', None, 'dp')
- grad_down: bfloat16 [16, 768, 2048], P('blk', 'dp')
Inputs may be any that keep to these rules, and one draw needn't show every extreme that they name: `block_expert`: the slots of device b (slots b * 14 to (b + 1) * 14 - 1) hold first between 1 and 7 blocks of expert b, then between 1 and 7 blocks of expert (b + 1) mod 16, then empty slots marked -1; device 0 holds 7 blocks of each of its two experts. `block_tokens`: indices into the 448 tokens of the slot's own device; the live blocks of one expert on one device name distinct tokens.
All inputs are finite; a program needn't handle non-finite values.
Results may differ from a plain program's by a relative error of at most 0.0066.
Values may be sent and summed in bfloat16 or wider, within the bound.
No kernel may reach another device: no remote copies, remote signals or barrier semaphores. Data moves between devices by JAX's collectives and lax.ppermute only.
A program may use at most 128 MiB of HBM per device.

v0:
```python
import jax
import jax.numpy as jnp
from jax import lax
from jax.sharding import PartitionSpec as P


def passed_along(block, axis, distance):
    size = lax.axis_size(axis)
    return lax.ppermute(block, axis, [((i - distance) % size, i) for i in range(size)])


def partner(block):
    return passed_along(block, "dp", 1)


def contract_rows(left_side, right_side):
    return lax.dot_general(
        left_side, right_side, (((1,), (1,)), ((), ())), preferred_element_type=jnp.float32
    )


def contract_cols(left_side, right_side):
    return lax.dot_general(
        left_side, right_side, (((0,), (0,)), ((), ())), preferred_element_type=jnp.float32
    )


def matmul(left_side, right_side):
    return jnp.dot(left_side, right_side, preferred_element_type=jnp.float32)


def forward(rows_in, w_first, w_second):
    gate_pre = matmul(rows_in, w_first)
    up_pre = matmul(rows_in, w_second)
    sigmoid_value = 1.0 / (1.0 + jnp.exp(-gate_pre))
    active = gate_pre * sigmoid_value
    slope_term = sigmoid_value * (1.0 + gate_pre * (1.0 - sigmoid_value))
    return active, slope_term, up_pre, (active * up_pre).astype(jnp.bfloat16)


def backward(scaled, w_third, active, slope_term, up_pre):
    back_hidden = contract_rows(scaled, w_third)
    grad_gate_pre = (back_hidden * up_pre * slope_term).astype(jnp.bfloat16)
    grad_up_pre = (back_hidden * active).astype(jnp.bfloat16)
    return grad_gate_pre, grad_up_pre


def rounded(values):
    return lax.optimization_barrier(values.astype(jnp.bfloat16)).astype(jnp.float32)


def on_device(tokens, cotangent, block_tokens, block_expert, block_gate, w_gate, w_up, w_down):
    size = lax.axis_size("blk")
    me = lax.axis_index("blk")
    half = lax.axis_index("dp")
    count, width = tokens.shape
    w_first, w_second, w_third = w_gate[0], w_up[0], w_down[0]

    def whole(mine, other):
        return jnp.where(
            half == 0,
            jnp.concatenate([mine, other], axis=1),
            jnp.concatenate([other, mine], axis=1),
        )

    def columns(weight, side):
        return lax.dynamic_slice_in_dim(weight, side * width, width, 1)

    def rows(weight, side):
        return lax.dynamic_slice_in_dim(weight, side * width, width, 0)

    def summed(part):
        return part(half) + partner(part(1 - half).astype(jnp.bfloat16)).astype(jnp.float32)

    gates = block_gate.astype(jnp.float32)
    hit = block_tokens.reshape(1, -1) == jnp.arange(count, dtype=jnp.int32)[:, None]

    def token_gate(expert):
        live = jnp.where((block_expert == expert)[:, None], gates, 0.0).reshape(1, -1)
        return jnp.sum(jnp.where(hit, live, 0.0), axis=1, keepdims=True)

    gate_own = token_gate(me)
    gate_next = token_gate(lax.rem(me + 1, size))

    guest_tokens = passed_along(tokens, "blk", 1)
    cot = cotangent.astype(jnp.float32)
    guest_scaled = passed_along((gate_next * cot).astype(jnp.bfloat16), "blk", 1)

    features = whole(tokens, partner(tokens))
    cotangents = whole(cotangent, partner(cotangent))
    scaled = (gate_own * cotangents.astype(jnp.float32)).astype(jnp.bfloat16)
    active, slope_term, up_pre, hidden = forward(features, w_first, w_second)
    own_out = gate_own * summed(lambda side: matmul(hidden, columns(w_third, side)))
    grad_one, grad_two = backward(scaled, w_third, active, slope_term, up_pre)
    own_back = summed(
        lambda side: contract_rows(grad_one, rows(w_first, side))
        + contract_rows(grad_two, rows(w_second, side))
    )
    own_grads = (
        contract_cols(features, grad_one),
        contract_cols(features, grad_two),
        contract_cols(hidden, scaled),
    )

    guest_features = whole(guest_tokens, partner(guest_tokens))
    active, slope_term, up_pre, guest_hidden = forward(guest_features, w_first, w_second)
    guest_out = summed(lambda side: matmul(guest_hidden, columns(w_third, side)))
    came_out = passed_along(guest_out.astype(jnp.bfloat16), "blk", -1)

    guest_cot = whole(guest_scaled, partner(guest_scaled))
    guest_one, guest_two = backward(guest_cot, w_third, active, slope_term, up_pre)
    guest_back = summed(
        lambda side: contract_rows(guest_one, rows(w_first, side))
        + contract_rows(guest_two, rows(w_second, side))
    )
    came_back = passed_along(guest_back.astype(jnp.bfloat16), "blk", -1)
    guest_grads = (
        contract_cols(guest_features, guest_one),
        contract_cols(guest_features, guest_two),
        contract_cols(guest_hidden, guest_cot),
    )

    outputs = own_out + gate_next * came_out.astype(jnp.float32)
    backs = own_back + came_back.astype(jnp.float32)
    grads = tuple(
        (rounded(own) + rounded(guest)).astype(jnp.bfloat16)[None]
        for own, guest in zip(own_grads, guest_grads)
    )
    return (outputs.astype(jnp.bfloat16), backs.astype(jnp.bfloat16)) + grads


def solution(mesh):
    in_specs = (
        P("blk", "dp"),
        P("blk", "dp"),
        P("blk", None),
        P("blk"),
        P("blk", None),
        P("blk", None, "dp"),
        P("blk", None, "dp"),
        P("blk", "dp", None),
    )
    out_specs = (
        P("blk", "dp"),
        P("blk", "dp"),
        P("blk", None, "dp"),
        P("blk", None, "dp"),
        P("blk", "dp", None),
    )
    return jax.shard_map(
        on_device, mesh=mesh, in_specs=in_specs, out_specs=out_specs, check_vma=False
    )
```

profile of v0, /device:TPU:0, one launch (start us, length us, event | category | flops | bytes accessed | tf_op | source)
XLA Modules:
  0.0 123.4 jit_solution(1403029441863046916)
XLA Ops:
  1.2 2.6 %collective-permute-start.2 = (bf16[448,1024]{1,0:T(8,128)(2,1)}, bf16[448,1024]{1,0:T(8,128)(2,1)}, u32[]{:S(2)}, u32[]{:S(2)}) collective-permute-start(bf16[448,1024]{1,0:T(8,128)(2,1)} %param.8), channel_id=1, source_target_pairs={{30,0},{0,2},{2,4},{4,6},{6,8},{8,10},{10,12},{12,14},{14,16},{16,... | collective-permute-start | bytes 2752520 | tf_op jit(solution)/shard_map/ppermute | solution.py:9
  3.9 0.8 eq.33
  5.3 0.8 convert_select_fusion
  6.8 2.3 %multiply_convert_fusion.1 = bf16[448,1024]{1,0:T(8,128)(2,1)} fusion(bf16[448,1024]{1,0:T(8,128)(2,1)} %param.9, f32[448]{0:T(512)S(1)} %get-tuple-element.6), kind=kLoop, calls=%fused_computation.17 | loop fusion | flops 1376256 | bytes 1836800 | tf_op jit(solution)/shard_map/convert_element_type | solution.py:87
  9.1 1.5 %collective-permute-start.8 = (bf16[448,1024]{1,0:T(8,128)(2,1)}, bf16[448,1024]{1,0:T(8,128)(2,1)}, u32[]{:S(2)}, u32[]{:S(2)}) collective-permute-start(bf16[448,1024]{1,0:T(8,128)(2,1)} %multiply_convert_fusion.1), channel_id=1, source_target_pairs={{30,0},{0,2},{2,4},{4,6},{6,8},{8,10},{10,12},{12,14},{14,16},{16,... | collective-permute-start | bytes 2752520 | tf_op jit(solution)/shard_map/ppermute | solution.py:9
  10.6 3.3 %fusion.9 = f32[448,384]{1,0:T(8,128)S(1)} fusion(bf16[1,2048,384]{2,1,0:T(8,128)(2,1)S(1)} %copy-done.2, bf16[448,1024]{1,0:T(8,128)(2,1)} %collective-permute-done, bf16[448,1024]{1,0:T(8,128)(2,1)} %param.8, pred[]{:T(512)S(6)} %eq.39), kind=kOutput, calls=%fused_computation.33 | convolution fusion | flops 712900608 | bytes 4096001 | tf_op jit(solution)/shard_map/dot_general | solution.py:29
  13.9 2.7 %fusion.13 = f32[448,384]{1,0:T(8,128)S(1)} fusion(bf16[1,2048,384]{2,1,0:T(8,128)(2,1)S(1)} %copy-done.1, bf16[448,1024]{1,0:T(8,128)(2,1)} %collective-permute-done, bf16[448,1024]{1,0:T(8,128)(2,1)S(1)} %copy-done.4, pred[]{:T(512)S(6)} %eq.39), kind=kOutput, calls=%fused_computation.37 | convolution fusion | flops 712900608 | bytes 4096001 | tf_op jit(solution)/shard_map/dot_general | solution.py:29
  16.6 2.9 %multiply_convert_fusion.4 = (bf16[448,384]{1,0:T(8,128)(2,1)S(1)}, bf16[448,384]{1,0:T(8,128)(2,1)S(1)}, bf16[448,384]{1,0:T(8,128)(2,1)S(1)}) fusion(f32[448,384]{1,0:T(8,128)S(1)} %fusion.13, f32[448,384]{1,0:T(8,128)S(1)} %fusion.9, bf16[1,384,2048]{2,1,0:T(8,128)(2,1)S(1)} %copy-done, bf16[448,1024]{1,0:T(8,128)(2,1)} %collective-permute-done.6, ...), kind=kOutput, calls=%fused_computation.74 | convolution fusion | flops 718233600 | bytes 5818113 | tf_op jit(solution)/shard_map/dot_general | solution.py:17
  20.3 0.7 fusion.19
  21.0 0.7 add_convert_fusion.6
  22.3 26.3 %collective-permute-done.8 = bf16[448,1024]{1,0:T(8,128)(2,1)} collective-permute-done((bf16[448,1024]{1,0:T(8,128)(2,1)}, bf16[448,1024]{1,0:T(8,128)(2,1)}, u32[]{:S(2)}, u32[]{:S(2)}) %collective-permute-start.8) | collective-permute-done | bytes 917536 | tf_op jit(solution)/shard_map/ppermute | solution.py:9
  48.7 2.6 %convolution_convert_fusion.1 = bf16[384,2048]{1,0:T(8,128)(2,1)S(1)} fusion(bf16[448,384]{1,0:T(8,128)(2,1)S(1)} %get-tuple-element.9, bf16[448,1024]{1,0:T(8,128)(2,1)} %collective-permute-done.6, bf16[448,1024]{1,0:T(8,128)(2,1)S(1)} %copy-done.3, f32[448]{0:T(512)S(1)} %get-tuple-element.5, pred[]{:T(512)S(6)} %eq.39), kind=kOutput, calls=%fused_computation.5 | convolution fusion | flops 716439552 | bytes 3753729 | tf_op jit(solution)/shard_map/dot_general | solution.py:23
  51.3 2.9 %convolution_convert_fusion.3 = bf16[2048,384]{1,0:T(8,128)(2,1)S(1)} fusion(bf16[448,384]{1,0:T(8,128)(2,1)S(1)} %get-tuple-element.7, bf16[448,1024]{1,0:T(8,128)(2,1)} %collective-permute-done, bf16[448,1024]{1,0:T(8,128)(2,1)S(1)} %copy-done.4, pred[]{:T(512)S(6)} %eq.39), kind=kOutput, calls=%fused_computation.7 | convolution fusion | flops 713687040 | bytes 3751937 | tf_op jit(solution)/shard_map/dot_general | solution.py:23
  55.4 2.9 %convolution_convert_fusion.5 = bf16[2048,384]{1,0:T(8,128)(2,1)S(1)} fusion(bf16[448,384]{1,0:T(8,128)(2,1)S(1)} %get-tuple-element.8, bf16[448,1024]{1,0:T(8,128)(2,1)} %collective-permute-done, bf16[448,1024]{1,0:T(8,128)(2,1)S(1)} %copy-done.4, pred[]{:T(512)S(6)} %eq.39), kind=kOutput, calls=%fused_computation.9 | convolution fusion | flops 713687040 | bytes 3751937 | tf_op jit(solution)/shard_map/dot_general | solution.py:23
  58.3 0.7 fusion.26
  59.0 2.6 %fusion.7 = f32[448,384]{1,0:T(8,128)S(1)} fusion(bf16[1,2048,384]{2,1,0:T(8,128)(2,1)S(1)} %copy-done.2, bf16[448,1024]{1,0:T(8,128)(2,1)S(1)} %collective-permute-done.3, bf16[448,1024]{1,0:T(8,128)(2,1)} %collective-permute-done.2, pred[]{:T(512)S(6)} %eq.39), kind=kOutput, calls=%fused_computation.31 | convolution fusion | flops 712900608 | bytes 4096001 | tf_op jit(solution)/shard_map/dot_general | solution.py:29
  61.6 2.6 %fusion.11 = f32[448,384]{1,0:T(8,128)S(1)} fusion(bf16[1,2048,384]{2,1,0:T(8,128)(2,1)S(1)} %copy-done.1, bf16[448,1024]{1,0:T(8,128)(2,1)S(1)} %collective-permute-done.3, bf16[448,1024]{1,0:T(8,128)(2,1)} %collective-permute-done.2, pred[]{:T(512)S(6)} %eq.39), kind=kOutput, calls=%fused_computation.35 | convolution fusion | flops 712900608 | bytes 4096001 | tf_op jit(solution)/shard_map/dot_general | solution.py:29
  64.2 3.0 %multiply_convert_fusion.2 = (bf16[448,384]{1,0:T(8,128)(2,1)S(1)}, bf16[448,384]{1,0:T(8,128)(2,1)S(1)}, bf16[448,384]{1,0:T(8,128)(2,1)S(1)}) fusion(f32[448,384]{1,0:T(8,128)S(1)} %fusion.11, f32[448,384]{1,0:T(8,128)S(1)} %fusion.7, bf16[1,384,2048]{2,1,0:T(8,128)(2,1)S(1)} %copy-done, bf16[448,1024]{1,0:T(8,128)(2,1)S(1)} %collective-permute-done.9, ...), kind=kOutput, calls=%fused_computation.72 | convolution fusion | flops 715481088 | bytes 5816321 | tf_op jit(solution)/shard_map/dot_general | solution.py:17
  69.1 2.8 %convolution_convert_fusion.4 = bf16[2048,384]{1,0:T(8,128)(2,1)S(1)} fusion(bf16[448,384]{1,0:T(8,128)(2,1)S(1)} %get-tuple-element.11, bf16[448,1024]{1,0:T(8,128)(2,1)S(1)} %collective-permute-done.3, bf16[448,1024]{1,0:T(8,128)(2,1)} %collective-permute-done.2, pred[]{:T(512)S(6)} %eq.39), kind=kOutput, calls=%fused_computation.8 | convolution fusion | flops 713687040 | bytes 3751937 | tf_op jit(solution)/shard_map/dot_general | solution.py:23
  71.9 2.8 %convolution_convert_fusion.2 = bf16[2048,384]{1,0:T(8,128)(2,1)S(1)} fusion(bf16[448,384]{1,0:T(8,128)(2,1)S(1)} %get-tuple-element.10, bf16[448,1024]{1,0:T(8,128)(2,1)S(1)} %collective-permute-done.3, bf16[448,1024]{1,0:T(8,128)(2,1)} %collective-permute-done.2, pred[]{:T(512)S(6)} %eq.39), kind=kOutput, calls=%fused_computation.6 | convolution fusion | flops 713687040 | bytes 3751937 | tf_op jit(solution)/shard_map/dot_general | solution.py:23
  74.7 0.7 add_convert_fusion.5
  75.4 0.7 fusion.24
  76.1 2.5 %fusion = (bf16[1,2048,384]{2,1,0:T(8,128)(2,1)}, bf16[1,2048,384]{2,1,0:T(8,128)(2,1)}) fusion(bf16[2048,384]{1,0:T(8,128)(2,1)S(1)} %convolution_convert_fusion.4, bf16[2048,384]{1,0:T(8,128)(2,1)S(1)} %convolution_convert_fusion.5, bf16[2048,384]{1,0:T(8,128)(2,1)S(1)} %convolution_convert_fusion.2, bf16[2048,384]{1,0:T(8,128)(2,1)S(1)} %convolution_convert_fusion.3), kind=kLoop, calls=%fused_computation.24 | loop fusion | flops 6291456 | bytes 9437184 | tf_op jit(solution)/shard_map/broadcast_in_dim | solution.py:126
  79.3 1.8 %collective-permute-start.5 = (bf16[448,1024]{1,0:T(8,128)(2,1)S(1)}, bf16[448,1024]{1,0:T(8,128)(2,1)S(1)}, u32[]{:S(2)}, u32[]{:S(2)}) collective-permute-start(bf16[448,1024]{1,0:T(8,128)(2,1)S(1)} %add_convert_fusion.8), channel_id=1, source_target_pairs={{2,0},{4,2},{6,4},{8,6},{10,8},{12,10},{14,12},{16,14},{18,16},{20... | collective-permute-start | bytes 2752520 | tf_op jit(solution)/shard_map/ppermute | solution.py:9
  81.1 0.7 add_convert_fusion.4
  81.8 1.5 %collective-permute-start.11 = (bf16[448,1024]{1,0:T(8,128)(2,1)S(1)}, bf16[448,1024]{1,0:T(8,128)(2,1)S(1)}, u32[]{:S(2)}, u32[]{:S(2)}) collective-permute-start(bf16[448,1024]{1,0:T(8,128)(2,1)S(1)} %add_convert_fusion.4), channel_id=1, source_target_pairs={{2,0},{4,2},{6,4},{8,6},{10,8},{12,10},{14,12},{16,14},{18,16},{20... | collective-permute-start | bytes 2752520 | tf_op jit(solution)/shard_map/ppermute | solution.py:9
  83.3 2.5 %convolution_convert_fusion = bf16[384,2048]{1,0:T(8,128)(2,1)S(1)} fusion(bf16[448,384]{1,0:T(8,128)(2,1)S(1)} %get-tuple-element.12, bf16[448,1024]{1,0:T(8,128)(2,1)S(1)} %collective-permute-done.9, bf16[448,1024]{1,0:T(8,128)(2,1)} %collective-permute-done.8, pred[]{:T(512)S(6)} %eq.39), kind=kOutput, calls=%fused_computation.4 | convolution fusion | flops 713687040 | bytes 3751937 | tf_op jit(solution)/shard_map/dot_general | solution.py:23
  85.8 1.7 %fusion.2 = bf16[1,384,2048]{2,1,0:T(8,128)(2,1)} fusion(bf16[384,2048]{1,0:T(8,128)(2,1)S(1)} %convolution_convert_fusion, bf16[384,2048]{1,0:T(8,128)(2,1)S(1)} %convolution_convert_fusion.1), kind=kLoop, calls=%fused_computation.26 | loop fusion | flops 3145728 | bytes 4718592 | tf_op jit(solution)/shard_map/broadcast_in_dim | solution.py:126
  87.6 14.9 %collective-permute-done.5 = bf16[448,1024]{1,0:T(8,128)(2,1)S(1)} collective-permute-done((bf16[448,1024]{1,0:T(8,128)(2,1)S(1)}, bf16[448,1024]{1,0:T(8,128)(2,1)S(1)}, u32[]{:S(2)}, u32[]{:S(2)}) %collective-permute-start.5) | collective-permute-done | bytes 917536 | tf_op jit(solution)/shard_map/ppermute | solution.py:9
  102.5 1.3 %add_convert_fusion.7 = bf16[448,1024]{1,0:T(8,128)(2,1)} fusion(bf16[448,1024]{1,0:T(8,128)(2,1)S(1)} %collective-permute-done.5, f32[448,1024]{1,0:T(8,128)S(1)} %fusion.32, bf16[448,1024]{1,0:T(8,128)(2,1)S(1)} %collective-permute-done.1, f32[448]{0:T(512)S(1)} %get-tuple-element.6, f32[448]{0:T(512)S(1)} %get-tuple-element.5), kind=kLoop, calls=%fused_computation.19 | loop fusion | flops 3211264 | bytes 4591104 | tf_op jit(solution)/shard_map/convert_element_type | solution.py:129
  103.8 17.9 %collective-permute-done.11 = bf16[448,1024]{1,0:T(8,128)(2,1)S(1)} collective-permute-done((bf16[448,1024]{1,0:T(8,128)(2,1)S(1)}, bf16[448,1024]{1,0:T(8,128)(2,1)S(1)}, u32[]{:S(2)}, u32[]{:S(2)}) %collective-permute-start.11) | collective-permute-done | bytes 917536 | tf_op jit(solution)/shard_map/ppermute | solution.py:9
  121.8 1.6 %add_convert_fusion.3 = bf16[448,1024]{1,0:T(8,128)(2,1)} fusion(bf16[448,1024]{1,0:T(8,128)(2,1)S(1)} %collective-permute-done.11, bf16[448,1024]{1,0:T(8,128)(2,1)S(1)} %collective-permute-done.7, f32[448,1024]{1,0:T(8,128)S(1)} %fusion.26, f32[448,1024]{1,0:T(8,128)S(1)} %fusion.22), kind=kLoop, calls=%fused_computation.14 | loop fusion | flops 2752512 | bytes 6422528 | tf_op jit(solution)/shard_map/convert_element_type | solution.py:129
  (37 shorter events, 7.4 us)
Async XLA Ops:
  0.6 15.9 %copy-start = (bf16[1,384,2048]{2,1,0:T(8,128)(2,1)S(1)}, bf16[1,384,2048]{2,1,0:T(8,128)(2,1)}, u32[]{:S(2)}) copy-start(bf16[1,384,2048]{2,1,0:T(8,128)(2,1)} %param.15) | copy-start | bytes 4718596
  0.6 9.9 %copy-start.2 = (bf16[1,2048,384]{2,1,0:T(8,128)(2,1)S(1)}, bf16[1,2048,384]{2,1,0:T(8,128)(2,1)}, u32[]{:S(2)}) copy-start(bf16[1,2048,384]{2,1,0:T(8,128)(2,1)} %param.14) | copy-start | bytes 4718596
  0.7 9.9 %collective-permute-start = (bf16[448,1024]{1,0:T(8,128)(2,1)}, bf16[448,1024]{1,0:T(8,128)(2,1)}, u32[]{:S(2)}, u32[]{:S(2)}) collective-permute-start(bf16[448,1024]{1,0:T(8,128)(2,1)} %param.8), channel_id=1, source_target_pairs={{1,0},{0,1},{3,2},{2,3},{5,4},{4,5},{7,6},{6,7},{9,8},{8,9},{11,10... | collective-permute-start | bytes 2752520 | tf_op jit(solution)/shard_map/ppermute | solution.py:9
  1.2 53.0 %collective-permute-start.2 = (bf16[448,1024]{1,0:T(8,128)(2,1)}, bf16[448,1024]{1,0:T(8,128)(2,1)}, u32[]{:S(2)}, u32[]{:S(2)}) collective-permute-start(bf16[448,1024]{1,0:T(8,128)(2,1)} %param.8), channel_id=1, source_target_pairs={{30,0},{0,2},{2,4},{4,6},{6,8},{8,10},{10,12},{12,14},{14,16},{16,... | collective-permute-start | bytes 2752520 | tf_op jit(solution)/shard_map/ppermute | solution.py:9
  3.7 12.8 %collective-permute-start.6 = (bf16[448,1024]{1,0:T(8,128)(2,1)}, bf16[448,1024]{1,0:T(8,128)(2,1)}, u32[]{:S(2)}, u32[]{:S(2)}) collective-permute-start(bf16[448,1024]{1,0:T(8,128)(2,1)} %param.9), channel_id=1, source_target_pairs={{1,0},{0,1},{3,2},{2,3},{5,4},{4,5},{7,6},{6,7},{9,8},{8,9},{11,10... | collective-permute-start | bytes 2752520 | tf_op jit(solution)/shard_map/ppermute | solution.py:9
  9.1 39.6 %collective-permute-start.8 = (bf16[448,1024]{1,0:T(8,128)(2,1)}, bf16[448,1024]{1,0:T(8,128)(2,1)}, u32[]{:S(2)}, u32[]{:S(2)}) collective-permute-start(bf16[448,1024]{1,0:T(8,128)(2,1)} %multiply_convert_fusion.1), channel_id=1, source_target_pairs={{30,0},{0,2},{2,4},{4,6},{6,8},{8,10},{10,12},{12,14},{14,16},{16,... | collective-permute-start | bytes 2752520 | tf_op jit(solution)/shard_map/ppermute | solution.py:9
  10.6 3.3 %copy-start.1 = (bf16[1,2048,384]{2,1,0:T(8,128)(2,1)S(1)}, bf16[1,2048,384]{2,1,0:T(8,128)(2,1)}, u32[]{:S(2)}) copy-start(bf16[1,2048,384]{2,1,0:T(8,128)(2,1)} %param.13) | copy-start | bytes 4718596
  10.6 3.3 %copy-start.4 = (bf16[448,1024]{1,0:T(8,128)(2,1)S(1)}, bf16[448,1024]{1,0:T(8,128)(2,1)}, u32[]{:S(2)}) copy-start(bf16[448,1024]{1,0:T(8,128)(2,1)} %param.8) | copy-start | bytes 2752516
  13.9 2.7 %copy-start.3 = (bf16[448,1024]{1,0:T(8,128)(2,1)S(1)}, bf16[448,1024]{1,0:T(8,128)(2,1)}, u32[]{:S(2)}) copy-start(bf16[448,1024]{1,0:T(8,128)(2,1)} %param.9) | copy-start | bytes 2752516
  20.2 67.4 %collective-permute-start.1 = (bf16[448,1024]{1,0:T(8,128)(2,1)S(1)}, bf16[448,1024]{1,0:T(8,128)(2,1)S(1)}, u32[]{:S(2)}, u32[]{:S(2)}) collective-permute-start(bf16[448,1024]{1,0:T(8,128)(2,1)S(1)} %convolution_convert_fusion.7), channel_id=1, source_target_pairs={{1,0},{0,1},{3,2},{2,3},{5,4},{4,5},{7,6},{6,7},{9,8},{8,9},{11,10... | collective-permute-start | bytes 2752520 | tf_op jit(solution)/shard_map/ppermute | solution.py:9
  48.7 15.6 %collective-permute-start.9 = (bf16[448,1024]{1,0:T(8,128)(2,1)}, bf16[448,1024]{1,0:T(8,128)(2,1)S(1)}, u32[]{:S(2)}, u32[]{:S(2)}) collective-permute-start(bf16[448,1024]{1,0:T(8,128)(2,1)} %collective-permute-done.8), channel_id=1, source_target_pairs={{1,0},{0,1},{3,2},{2,3},{5,4},{4,5},{7,6},{6,7},{9,8},{8,9},{11,10... | collective-permute-start | bytes 2752520 | tf_op jit(solution)/shard_map/ppermute | solution.py:9
  54.2 4.9 %collective-permute-start.3 = (bf16[448,1024]{1,0:T(8,128)(2,1)}, bf16[448,1024]{1,0:T(8,128)(2,1)S(1)}, u32[]{:S(2)}, u32[]{:S(2)}) collective-permute-start(bf16[448,1024]{1,0:T(8,128)(2,1)} %collective-permute-done.2), channel_id=1, source_target_pairs={{1,0},{0,1},{3,2},{2,3},{5,4},{4,5},{7,6},{6,7},{9,8},{8,9},{11,10... | collective-permute-start | bytes 2752520 | tf_op jit(solution)/shard_map/ppermute | solution.py:9
  59.0 44.9 %collective-permute-start.7 = (bf16[448,1024]{1,0:T(8,128)(2,1)S(1)}, bf16[448,1024]{1,0:T(8,128)(2,1)S(1)}, u32[]{:S(2)}, u32[]{:S(2)}) collective-permute-start(bf16[448,1024]{1,0:T(8,128)(2,1)S(1)} %add_convert_fusion.6), channel_id=1, source_target_pairs={{1,0},{0,1},{3,2},{2,3},{5,4},{4,5},{7,6},{6,7},{9,8},{8,9},{11,10... | collective-permute-start | bytes 2752520 | tf_op jit(solution)/shard_map/ppermute | solution.py:9
  67.9 10.8 %collective-permute-start.4 = (bf16[448,1024]{1,0:T(8,128)(2,1)S(1)}, bf16[448,1024]{1,0:T(8,128)(2,1)S(1)}, u32[]{:S(2)}, u32[]{:S(2)}) collective-permute-start(bf16[448,1024]{1,0:T(8,128)(2,1)S(1)} %convolution_convert_fusion.6), channel_id=1, source_target_pairs={{1,0},{0,1},{3,2},{2,3},{5,4},{4,5},{7,6},{6,7},{9,8},{8,9},{11,10... | collective-permute-start | bytes 2752520 | tf_op jit(solution)/shard_map/ppermute | solution.py:9
  75.3 5.8 %collective-permute-start.10 = (bf16[448,1024]{1,0:T(8,128)(2,1)S(1)}, bf16[448,1024]{1,0:T(8,128)(2,1)S(1)}, u32[]{:S(2)}, u32[]{:S(2)}) collective-permute-start(bf16[448,1024]{1,0:T(8,128)(2,1)S(1)} %add_convert_fusion.5), channel_id=1, source_target_pairs={{1,0},{0,1},{3,2},{2,3},{5,4},{4,5},{7,6},{6,7},{9,8},{8,9},{11,10... | collective-permute-start | bytes 2752520 | tf_op jit(solution)/shard_map/ppermute | solution.py:9
  79.3 23.2 %collective-permute-start.5 = (bf16[448,1024]{1,0:T(8,128)(2,1)S(1)}, bf16[448,1024]{1,0:T(8,128)(2,1)S(1)}, u32[]{:S(2)}, u32[]{:S(2)}) collective-permute-start(bf16[448,1024]{1,0:T(8,128)(2,1)S(1)} %add_convert_fusion.8), channel_id=1, source_target_pairs={{2,0},{4,2},{6,4},{8,6},{10,8},{12,10},{14,12},{16,14},{18,16},{20... | collective-permute-start | bytes 2752520 | tf_op jit(solution)/shard_map/ppermute | solution.py:9
  81.8 40.0 %collective-permute-start.11 = (bf16[448,1024]{1,0:T(8,128)(2,1)S(1)}, bf16[448,1024]{1,0:T(8,128)(2,1)S(1)}, u32[]{:S(2)}, u32[]{:S(2)}) collective-permute-start(bf16[448,1024]{1,0:T(8,128)(2,1)S(1)} %add_convert_fusion.4), channel_id=1, source_target_pairs={{2,0},{4,2},{6,4},{8,6},{10,8},{12,10},{14,12},{16,14},{18,16},{20... | collective-permute-start | bytes 2752520 | tf_op jit(solution)/shard_map/ppermute | solution.py:9
where the time goes:
time: 124 us; the launch traced here: 123 us
  waiting for transfers between devices  59.2 us (48%)
  matrix products  41.4 us (33%)
  other arithmetic  11.5 us (9%)
  starting transfers between devices  9.45 us (8%)
    ppermute x12, waiting for transfers between devices, passed_along(): lax.ppermute(block, axis, [((i - distance) % size, i) for i in range(size)])  59.2 us
    dot_general x6, matrix products, contract_cols(): lax.dot_general(left_side, right_side, (((0,), (0,)), ((), ())), preferre...  16.4 us
    dot_general x8, matrix products, matmul(): return jnp.dot(left_side, right_side, preferred_element_type=jnp.float32)  13.7 us
    dot_general x10, matrix products, contract_rows(): lax.dot_general(left_side, right_side, (((1,), (1,)), ((), ())), preferre...  11.3 us
    ppermute x12, starting transfers between devices, passed_along(): lax.ppermute(block, axis, [((i - distance) % size, i) for i in range(size)])  9.45 us
    broadcast_in_dim x2, other arithmetic, on_device(): (rounded(own) + rounded(guest)).astype(jnp.bfloat16)[None]  4.28 us
    convert_element_type x2, other arithmetic, on_device(): return (outputs.astype(jnp.bfloat16), backs.astype(jnp.bfloat16)) + grads  2.94 us
  transfers between devices with their start and end apart: 12, of which 3 were waited for; matrix products, arithmetic and copies ran while one was open for 42% of the time, Pallas kernels for 0%

commit v1 on v0

v1 whole, which is shorter than its diff:
```python
import jax
import jax.numpy as jnp
from jax import lax
from jax.experimental import pallas as pl
from jax.experimental.pallas import tpu as pltpu
from jax.sharding import PartitionSpec as P

BF16 = jnp.bfloat16
F32 = jnp.float32
VMEM = pl.BlockSpec(memory_space=pltpu.VMEM)
SMEM = pl.BlockSpec(memory_space=pltpu.SMEM)
ANY = pl.BlockSpec(memory_space=pl.ANY)


def passed_along(block, axis, distance):
    size = lax.axis_size(axis)
    return lax.ppermute(block, axis, [((i - distance) % size, i) for i in range(size)])


def partner(block, pieces=1):
    if pieces == 1:
        return passed_along(block, "dp", 1)
    step = block.shape[0] // pieces
    swapped = [
        passed_along(block[i * step : (i + 1) * step], "dp", 1) for i in range(pieces)
    ]
    return jnp.concatenate(swapped, axis=0)


def matmul(left_side, right_side):
    return jnp.dot(left_side, right_side, preferred_element_type=F32)


def contract_rows(left_side, right_side):
    return lax.dot_general(
        left_side, right_side, (((1,), (1,)), ((), ())), preferred_element_type=F32
    )


def contract_cols(left_side, right_side):
    return lax.dot_general(
        left_side, right_side, (((0,), (0,)), ((), ())), preferred_element_type=F32
    )


def call(body, outs, specs, *operands, name, limit=48, flops=1):
    return pl.pallas_call(
        body,
        out_shape=[jax.ShapeDtypeStruct(shape, kind) for shape, kind in outs],
        in_specs=specs,
        out_specs=[VMEM] * len(outs),
        compiler_params=pltpu.CompilerParams(vmem_limit_bytes=limit * 2**20),
        cost_estimate=pl.CostEstimate(flops=flops, bytes_accessed=1, transcendentals=0),
        name=name,
    )(*operands)


def after(block, ready):
    return pl.pallas_call(
        lambda *refs: None,
        out_shape=jax.ShapeDtypeStruct(block.shape, block.dtype),
        in_specs=[ANY, ANY],
        out_specs=ANY,
        input_output_aliases={0: 0},
        compiler_params=pltpu.CompilerParams(vmem_limit_bytes=2**20),
        cost_estimate=pl.CostEstimate(flops=1, bytes_accessed=1, transcendentals=0),
        name="after",
    )(block, ready)


def sides(place, width):
    half = place[2]
    mine = pl.ds(pl.multiple_of(half * width, width), width)
    other = pl.ds(pl.multiple_of((1 - half) * width, width), width)
    return mine, other


def gates_body(place, slot_expert, slot_tokens, slot_gate, cot, gate_own, gate_next, scaled):
    slots, block = slot_tokens.shape
    count = cot.shape[0]
    token = lax.broadcasted_iota(jnp.int32, (count, block), 0)
    own = jnp.zeros((count, block), F32)
    following = jnp.zeros((count, block), F32)
    for slot in range(slots):
        expert = slot_expert[slot]
        gates = slot_gate[pl.ds(slot, 1), :]
        hit = token == slot_tokens[pl.ds(slot, 1), :]
        own += jnp.where(hit, jnp.where(expert == place[0], gates, 0.0), 0.0)
        following += jnp.where(hit, jnp.where(expert == place[1], gates, 0.0), 0.0)
    gate_own[...] = jnp.sum(own, axis=1, keepdims=True)
    column = jnp.sum(following, axis=1, keepdims=True)
    gate_next[...] = column
    scaled[...] = (column * cot[...].astype(F32)).astype(BF16)


def forward(tok_mine, tok_other, w_first, w_second, mine, other):
    gate_pre = matmul(tok_mine, w_first[mine, :]) + matmul(tok_other, w_first[other, :])
    up_pre = matmul(tok_mine, w_second[mine, :]) + matmul(tok_other, w_second[other, :])
    sigmoid_value = 1.0 / (1.0 + jnp.exp(-gate_pre))
    active = gate_pre * sigmoid_value
    slope_term = sigmoid_value * (1.0 + gate_pre * (1.0 - sigmoid_value))
    return active, up_pre * slope_term, (active * up_pre).astype(BF16)


def backward(cot_mine, cot_other, w_third, mine, other, active, slope_up):
    back_hidden = contract_rows(cot_mine, w_third[:, mine]) + contract_rows(
        cot_other, w_third[:, other]
    )
    return (back_hidden * slope_up).astype(BF16), (back_hidden * active).astype(BF16)


def back_rows(grad_one, grad_two, w_first, w_second, side):
    return contract_rows(grad_one, w_first[side, :]) + contract_rows(grad_two, w_second[side, :])


def own_body(
    place, tok_m, tok_o, cot_m, cot_o, gate, w_first, w_second, w_third,
    out_send, out_keep, back_send, back_keep, grad_first, grad_second, grad_third,
):
    mine, other = sides(place, tok_m.shape[1])
    active, slope_up, hidden = forward(tok_m[...], tok_o[...], w_first, w_second, mine, other)
    column = gate[...]
    out_send[...] = (column * matmul(hidden, w_third[:, other])).astype(BF16)
    out_keep[...] = column * matmul(hidden, w_third[:, mine])
    scaled_m = (column * cot_m[...].astype(F32)).astype(BF16)
    scaled_o = (column * cot_o[...].astype(F32)).astype(BF16)
    one, two = backward(scaled_m, scaled_o, w_third, mine, other, active, slope_up)
    back_send[...] = back_rows(one, two, w_first, w_second, other).astype(BF16)
    back_keep[...] = back_rows(one, two, w_first, w_second, mine)
    grad_first[mine, :] = contract_cols(tok_m[...], one).astype(BF16)
    grad_first[other, :] = contract_cols(tok_o[...], one).astype(BF16)
    grad_second[mine, :] = contract_cols(tok_m[...], two).astype(BF16)
    grad_second[other, :] = contract_cols(tok_o[...], two).astype(BF16)
    grad_third[:, mine] = contract_cols(hidden, scaled_m).astype(BF16)
    grad_third[:, other] = contract_cols(hidden, scaled_o).astype(BF16)


def guest_forward_body(
    place, tok_m, tok_o, w_first, w_second, w_third,
    out_send, out_keep, active_ref, slope_ref, hidden_ref,
):
    mine, other = sides(place, tok_m.shape[1])
    active, slope_up, hidden = forward(tok_m[...], tok_o[...], w_first, w_second, mine, other)
    out_send[...] = matmul(hidden, w_third[:, other]).astype(BF16)
    out_keep[...] = matmul(hidden, w_third[:, mine])
    active_ref[...] = active
    slope_ref[...] = slope_up
    hidden_ref[...] = hidden


def guest_backward_body(
    place, cot_m, cot_o, w_first, w_second, w_third, active, slope_up,
    back_send, back_keep, one_ref, two_ref,
):
    mine, other = sides(place, cot_m.shape[1])
    one, two = backward(cot_m[...], cot_o[...], w_third, mine, other, active[...], slope_up[...])
    back_send[...] = back_rows(one, two, w_first, w_second, other).astype(BF16)
    back_keep[...] = back_rows(one, two, w_first, w_second, mine)
    one_ref[...] = one
    two_ref[...] = two


def grads_body(
    place, tok_m, tok_o, cot_m, cot_o, hidden, one, two, own_first, own_second, own_third, *rest
):
    grad_first, grad_second, grad_third = rest[-3:]
    mine, other = sides(place, tok_m.shape[1])

    def joined(own, lent):
        return (own.astype(F32) + lent.astype(BF16).astype(F32)).astype(BF16)

    for side, tok, cot in ((mine, tok_m, cot_m), (other, tok_o, cot_o)):
        grad_first[0, side, :] = joined(own_first[side, :], contract_cols(tok[...], one[...]))
        grad_second[0, side, :] = joined(own_second[side, :], contract_cols(tok[...], two[...]))
        grad_third[0, :, side] = joined(own_third[:, side], contract_cols(hidden[...], cot[...]))


def on_device(tokens, cotangent, block_tokens, block_expert, block_gate, w_gate, w_up, w_down):
    size = lax.axis_size("blk")
    me = lax.axis_index("blk")
    place = jnp.stack([me, lax.rem(me + 1, size), lax.axis_index("dp")]).astype(jnp.int32)
    weights = (w_gate[0], w_up[0], w_down[0])
    rows = (tokens.shape, F32)
    rows16 = (tokens.shape, BF16)
    units = (tokens.shape[0], w_down.shape[1])
    column = ((tokens.shape[0], 1), F32)

    guest_tokens = passed_along(tokens, "blk", 1)
    gate_own, gate_next, scaled_next = call(
        gates_body, [column, column, rows16], [SMEM, SMEM, VMEM, VMEM, VMEM],
        place, block_expert, block_tokens, block_gate.astype(F32), cotangent,
        name="gates",
    )
    guest_cot = passed_along(scaled_next, "blk", 1)

    out_send, out_keep, back_send, back_keep, *own_grads = call(
        own_body,
        [rows16, rows, rows16, rows] + [(weight.shape, BF16) for weight in weights],
        [SMEM] + [VMEM] * 8,
        place, tokens, partner(tokens), cotangent, partner(cotangent), gate_own, *weights,
        name="own",
    )
    own_out = out_keep + partner(out_send).astype(F32)
    own_back = back_keep + partner(back_send).astype(F32)

    guest_tokens = after(guest_tokens, out_send)
    guest_other = partner(guest_tokens, 4)
    lent_send, lent_keep, active, slope_up, hidden = call(
        guest_forward_body,
        [rows16, rows, (units, F32), (units, F32), (units, BF16)],
        [SMEM] + [VMEM] * 5,
        place, guest_tokens, guest_other, *weights,
        name="guest_forward",
    )
    lent_out = (lent_keep + partner(lent_send, 4).astype(F32)).astype(BF16)
    came_out = passed_along(lent_out, "blk", -1)

    guest_cot = after(guest_cot, lent_out)
    cot_other = partner(guest_cot, 4)
    lent_send, lent_keep, one, two = call(
        guest_backward_body,
        [rows16, rows, (units, BF16), (units, BF16)],
        [SMEM] + [VMEM] * 7,
        place, guest_cot, cot_other, *weights, active, slope_up,
        name="guest_backward",
    )
    lent_back = (lent_keep + partner(lent_send, 2).astype(F32)).astype(BF16)
    came_back = passed_along(lent_back, "blk", -1)
    outputs = (own_out + gate_next * came_out.astype(F32)).astype(BF16)
    grads = call(
        grads_body,
        [(weight.shape, BF16) for weight in (w_gate, w_up, w_down)],
        [SMEM] + [VMEM] * 10 + [ANY, ANY],
        place, guest_tokens, guest_other, guest_cot, cot_other, hidden, one, two, *own_grads,
        lent_back, outputs,
        name="grads", flops=30*10**9,
    )
    backs = own_back + came_back.astype(F32)
    return (outputs, backs.astype(BF16), *grads)


def solution(mesh):
    in_specs = (
        P("blk", "dp"),
        P("blk", "dp"),
        P("blk", None),
        P("blk"),
        P("blk", None),
        P("blk", None, "dp"),
        P("blk", None, "dp"),
        P("blk", "dp", None),
    )
    out_specs = (
        P("blk", "dp"),
        P("blk", "dp"),
        P("blk", None, "dp"),
        P("blk", None, "dp"),
        P("blk", "dp", None),
    )
    return jax.shard_map(
        on_device, mesh=mesh, in_specs=in_specs, out_specs=out_specs, check_vma=False
    )
```

time: 124 us -> 100 us (0.81)
  matrix products: 41.4 us -> 0 us
  Pallas kernels: 0 us -> 34.9 us
  waiting for transfers between devices: 59.2 us -> 42.6 us
  local copies, waits for them, and re-layouts: 0.93 us -> 6.36 us
  other arithmetic: 11.5 us -> 7.6 us
  starting transfers between devices: 9.45 us -> 7.71 us
    dot_general x24 -> x0, matrix products: 41.4 us -> none  [the longest x6 16.4 us: contract_cols(): lax.dot_general(left_side, right_side, (((0,), (0,)), ((), ())), preferre...]
    pallas_call x0 -> x7, Pallas kernels: none -> 34.9 us  [the longest x5 34.9 us: call(): pl.pallas_call(body, out_shape=[jax.ShapeDtypeStruct(shape, kind) for sha...]
    ppermute x12 -> x22, waiting for transfers between devices: 59.2 us -> 42.6 us  [passed_along(): lax.ppermute(block, axis, [((i - distance) % size, i) for i in range(size)])]
    unnamed x10 -> x42, local copies, waits for them, and re-layouts: 0.03 us -> 5.12 us
    broadcast_in_dim x2 -> x0, other arithmetic: 4.28 us -> none  [on_device(): (rounded(own) + rounded(guest)).astype(jnp.bfloat16)[None]]
    convert_element_type x3 -> x5, other arithmetic: 5.26 us -> 7.38 us  [the longest x1 2.89 us: on_device(): outputs = (own_out + gate_next * came_out.astype(F32)).astype(BF16)]
    ppermute x12 -> x22, starting transfers between devices: 9.45 us -> 7.71 us  [passed_along(): lax.ppermute(block, axis, [((i - distance) % size, i) for i in range(size)])]
  transfers between devices with their start and end apart: 12 -> 22, of which waited for: 3 -> 18; matrix products, arithmetic and copies ran while one was open for 42% -> 7% of each run, Pallas kernels for 0% -> 35%
where the time goes in v1:
time: 100 us
  waiting for transfers between devices  42.6 us (43%)
  Pallas kernels  34.9 us (35%)
  starting transfers between devices  7.71 us (8%)
  other arithmetic  7.6 us (8%)
  local copies, waits for them, and re-layouts  6.36 us (6%)
    ppermute x22, waiting for transfers between devices, passed_along(): lax.ppermute(block, axis, [((i - distance) % size, i) for i in range(size)])  42.6 us
    pallas_call x5, Pallas kernels, call(): pl.pallas_call(body, out_shape=[jax.ShapeDtypeStruct(shape, kind) for sha...  34.9 us
    ppermute x22, starting transfers between devices, passed_along(): lax.ppermute(block, axis, [((i - distance) % size, i) for i in range(size)])  7.71 us
    unnamed x42, local copies, waits for them, and re-layouts  5.12 us
    convert_element_type x1, other arithmetic, on_device(): outputs = (own_out + gate_next * came_out.astype(F32)).astype(BF16)  2.89 us
    convert_element_type x1, other arithmetic, on_device(): lent_back = (lent_keep + partner(lent_send, 2).astype(F32)).astype(BF16)  2.14 us
  transfers between devices with their start and end apart: 22, of which 18 were waited for; matrix products, arithmetic and copies ran while one was open for 7% of the time, Pallas kernels for 35%

profile of v1, /device:TPU:0, one launch (start us, length us, event | category | flops | bytes accessed | tf_op | source)
XLA Modules:
  0.0 100.1 jit_solution(16814743232521036123)
XLA Ops:
  0.6 0.5 collective-permute-start
  1.2 2.9 %collective-permute-start.3 = (bf16[448,1024]{1,0:T(8,128)(2,1)}, bf16[448,1024]{1,0:T(8,128)(2,1)S(1)}, u32[]{:S(2)}, u32[]{:S(2)}) collective-permute-start(bf16[448,1024]{1,0:T(8,128)(2,1)} %tok_m.1), channel_id=1, source_target_pairs={{30,0},{0,2},{2,4},{4,6},{6,8},{8,10},{10,12},{12,14},{14,16},{16,... | collective-permute-start | bytes 2752520 | tf_op jit(solution)/shard_map/ppermute | solution.py:17
  4.1 0.7 convert_element_type.33.slot_gate
  4.9 1.2 %copy-done.1 = bf16[448,1024]{1,0:T(8,128)(2,1)S(1)} copy-done((bf16[448,1024]{1,0:T(8,128)(2,1)S(1)}, bf16[448,1024]{1,0:T(8,128)(2,1)}, u32[]{:S(2)}) %copy-start.1) | copy-done | bytes 917528
  6.1 0.7 copy-done.8
  6.8 0.7 copy-done.9
  7.4 1.6 %gates.1 = (f32[448,1]{1,0:T(8,128)S(1)}, f32[448,1]{1,0:T(8,128)S(1)}, bf16[448,1024]{1,0:T(8,128)(2,1)S(1)}) custom-call(s32[3]{0:T(128)S(1)} %pad_add_fusion.place, s32[14]{0:T(128)S(1)} %copy-done.9, s32[14,64]{1,0:T(8,128)S(1)} %copy-done.8, f32[14,64]{1,0:T(8,128)S(1)} %convert_element_type.33.slot_gate, bf16[448,1024]{1,0:T(8,128)(2,1)S(1)} %copy-done.1), custom_call_target="tpu_custom_call" | custom-call | flops 1 | bytes 1 | tf_op jit(solution)/shard_map/gates/pallas_call | solution.py:47
  9.1 1.2 %copy-done.2 = bf16[448,1024]{1,0:T(8,128)(2,1)S(1)} copy-done((bf16[448,1024]{1,0:T(8,128)(2,1)S(1)}, bf16[448,1024]{1,0:T(8,128)(2,1)}, u32[]{:S(2)}) %copy-start.2) | copy-done | bytes 917528
  10.3 1.2 %copy-done.7 = bf16[448,1024]{1,0:T(8,128)(2,1)S(1)} copy-done((bf16[448,1024]{1,0:T(8,128)(2,1)S(1)}, bf16[448,1024]{1,0:T(8,128)(2,1)}, u32[]{:S(2)}) %copy-start.7) | copy-done | bytes 917528
  11.4 12.6 %own.1 = (bf16[448,1024]{1,0:T(8,128)(2,1)}, f32[448,1024]{1,0:T(8,128)}, bf16[448,1024]{1,0:T(8,128)(2,1)S(1)}, f32[448,1024]{1,0:T(8,128)}, bf16[2048,384]{1,0...) custom-call(s32[3]{0:T(128)S(1)} %pad_add_fusion.place, bf16[448,1024]{1,0:T(8,128)(2,1)S(1)} %copy-done.7, ...), custom_call_target="tpu_custom_call" | custom-call | flops 1 | bytes 1 | tf_op jit(solution)/shard_map/own/pallas_call | solution.py:47
  24.0 4.9 %collective-permute-done.3.refs_0_ = bf16[448,1024]{1,0:T(8,128)(2,1)S(1)} collective-permute-done((bf16[448,1024]{1,0:T(8,128)(2,1)}, bf16[448,1024]{1,0:T(8,128)(2,1)S(1)}, u32[]{:S(2)}, u32[]{:S(2)}) %collective-permute-start.3) | collective-permute-done | bytes 917536 | tf_op jit(solution)/shard_map/ppermute | solution.py:17
  29.1 0.5 collective-permute-start.5
  29.7 0.4 collective-permute-start.7
  30.1 0.5 collective-permute-done.4
  31.6 6.5 %guest_forward.1 = (bf16[448,1024]{1,0:T(8,128)(2,1)S(1)}, f32[448,1024]{1,0:T(8,128)}, f32[448,384]{1,0:T(8,128)S(1)}, f32[448,384]{1,0:T(8,128)S(1)}, bf16[448,384]{1,0:T(8,128)(2,1)S(1)}) custom-call(s32[3]{0:T(128)S(1)} %pad_add_fusion.place, bf16[448,1024]{1,0:T(8,128)(2,1)S(1)} %after.2.tok_m, ...), custom_call_target="tpu_custom_call" | custom-call | flops 1 | bytes 1 | tf_op jit(solution)/shard_map/guest_forward/pallas_call | solution.py:47
  39.3 0.5 collective-permute-done.11
  41.1 14.6 %collective-permute-done.14.refs_0_ = bf16[448,1024]{1,0:T(8,128)(2,1)S(1)} collective-permute-done((bf16[448,1024]{1,0:T(8,128)(2,1)S(1)}, bf16[448,1024]{1,0:T(8,128)(2,1)S(1)}, u32[]{:S(2)}, u32[]{:S(2)}) %collective-permute-start.14) | collective-permute-done | bytes 917536 | tf_op jit(solution)/shard_map/ppermute | solution.py:17
  55.8 0.5 collective-permute-start.16
  56.3 0.4 collective-permute-start.17
  56.8 0.5 collective-permute-done.15
  57.6 1.4 %collective-permute-done.17 = bf16[112,1024]{1,0:T(8,128)(2,1)S(1)} collective-permute-done((bf16[112,1024]{1,0:T(8,128)(2,1)S(1)}, bf16[112,1024]{1,0:T(8,128)(2,1)S(1)}, u32[]{:S(2)}, u32[]{:S(2)}) %collective-permute-start.17) | collective-permute-done | bytes 229408 | tf_op jit(solution)/shard_map/ppermute | solution.py:17
  59.0 0.5 collective-permute-done.18
  59.6 7.0 %guest_backward.1 = (bf16[448,1024]{1,0:T(8,128)(2,1)S(1)}, f32[448,1024]{1,0:T(8,128)}, bf16[448,384]{1,0:T(8,128)(2,1)S(1)}, bf16[448,384]{1,0:T(8,128)(2,1)S(1)}) custom-call(s32[3]{0:T(128)S(1)} %pad_add_fusion.place, bf16[448,1024]{1,0:T(8,128)(2,1)S(1)} %after.3.cot_m, bf16[448,1024]{1,0:T(8,128)(2,1)S(1)} %constant_dynamic-update-slice_fusion.4.cot_o, ...), custom_call_target="tpu_custom_call" | custom-call | flops 1 | bytes 1 | tf_op jit(solution)/shard_map/guest_backward/pallas_call | solution.py:47
  66.6 1.0 %fusion = (bf16[224,1024]{1,0:T(8,128)(2,1)}, bf16[224,1024]{1,0:T(8,128)(2,1)}) fusion(bf16[448,1024]{1,0:T(8,128)(2,1)S(1)} %get-tuple-element.39), kind=kLoop, calls=%fused_computation.13 | loop fusion | bytes 1835008 | tf_op jit(solution)/shard_map/slice | solution.py:25
  68.6 1.3 %collective-permute-done.20 = bf16[224,1024]{1,0:T(8,128)(2,1)} collective-permute-done((bf16[224,1024]{1,0:T(8,128)(2,1)}, bf16[224,1024]{1,0:T(8,128)(2,1)}, u32[]{:S(2)}, u32[]{:S(2)}) %collective-permute-start.20) | collective-permute-done | bytes 458784 | tf_op jit(solution)/shard_map/ppermute | solution.py:17
  69.9 0.7 collective-permute-done.19
  70.5 2.1 %add_convert_fusion.1.rest_0_ = bf16[448,1024]{1,0:T(8,128)(2,1)S(1)} fusion(f32[448,1024]{1,0:T(8,128)} %get-tuple-element.38, bf16[224,1024]{1,0:T(8,128)(2,1)} %collective-permute-done.20, bf16[224,1024]{1,0:T(8,128)(2,1)} %collective-permute-done.19), kind=kLoop, calls=%fused_computation.1 | loop fusion | flops 2752512 | bytes 3670016 | tf_op jit(solution)/shard_map/convert_element_type | solution.py:227
  72.8 6.8 %collective-permute-done.12 = bf16[448,1024]{1,0:T(8,128)(2,1)} collective-permute-done((bf16[448,1024]{1,0:T(8,128)(2,1)S(1)}, bf16[448,1024]{1,0:T(8,128)(2,1)}, u32[]{:S(2)}, u32[]{:S(2)}) %collective-permute-start.12) | collective-permute-done | bytes 917536 | tf_op jit(solution)/shard_map/ppermute | solution.py:17
  79.6 2.9 %add_convert_fusion.2.rest_1_ = bf16[448,1024]{1,0:T(8,128)(2,1)} fusion(bf16[448,1024]{1,0:T(8,128)(2,1)} %collective-permute-done.12, f32[448,1024]{1,0:T(8,128)S(1)} %copy-done.17, bf16[448,1024]{1,0:T(8,128)(2,1)} %collective-permute-done.2, f32[448]{0:T(512)S(1)} %reduce), kind=kLoop, calls=%fused_computation.2 | loop fusion | flops 2752512 | bytes 4589312 | tf_op jit(solution)/shard_map/convert_element_type | solution.py:229
  82.5 7.2 %grads.1 = (bf16[1,2048,384]{2,1,0:T(8,128)(2,1)}, bf16[1,2048,384]{2,1,0:T(8,128)(2,1)}, bf16[1,384,2048]{2,1,0:T(8,128)(2,1)}) custom-call(s32[3]{0:T(128)S(1)} %pad_add_fusion.place, bf16[448,1024]{1,0:T(8,128)(2,1)S(1)} %after.2.tok_m, bf16[448,1024]{1,0:T(8,128)(2,1)S(1)} %copy-done.4, bf16[448,1024]{1,0:T(8,128)(2,1)S(1)} %after.3.cot_m, ...), custom_call_target="tpu_custom_call" | custom-call | flops 30000001024 | bytes 1 | tf_op jit(solution)/shard_map/grads/pallas_call | solution.py:47
  89.7 8.9 %collective-permute-done.21 = bf16[448,1024]{1,0:T(8,128)(2,1)S(1)} collective-permute-done((bf16[448,1024]{1,0:T(8,128)(2,1)S(1)}, bf16[448,1024]{1,0:T(8,128)(2,1)S(1)}, u32[]{:S(2)}, u32[]{:S(2)}) %collective-permute-start.21) | collective-permute-done | bytes 917536 | tf_op jit(solution)/shard_map/ppermute | solution.py:17
  98.7 1.4 %add_convert_fusion = bf16[448,1024]{1,0:T(8,128)(2,1)} fusion(bf16[448,1024]{1,0:T(8,128)(2,1)S(1)} %collective-permute-done.21, f32[448,1024]{1,0:T(8,128)S(1)} %copy-done.15, bf16[448,1024]{1,0:T(8,128)(2,1)S(1)} %collective-permute-done.13), kind=kLoop, calls=%fused_computation | loop fusion | flops 2293760 | bytes 4587520 | tf_op jit(solution)/shard_map/convert_element_type | solution.py:239
  (74 shorter events, 5.5 us)
Async XLA Ops:
  0.6 8.4 %collective-permute-start = (bf16[448,1024]{1,0:T(8,128)(2,1)}, bf16[448,1024]{1,0:T(8,128)(2,1)S(1)}, u32[]{:S(2)}, u32[]{:S(2)}) collective-permute-start(bf16[448,1024]{1,0:T(8,128)(2,1)} %tok_m.1), channel_id=1, source_target_pairs={{1,0},{0,1},{3,2},{2,3},{5,4},{4,5},{7,6},{6,7},{9,8},{8,9},{11,10... | collective-permute-start | bytes 2752520 | tf_op jit(solution)/shard_map/ppermute | solution.py:17
  1.1 7.9 %collective-permute-start.1 = (bf16[448,1024]{1,0:T(8,128)(2,1)}, bf16[448,1024]{1,0:T(8,128)(2,1)S(1)}, u32[]{:S(2)}, u32[]{:S(2)}) collective-permute-start(bf16[448,1024]{1,0:T(8,128)(2,1)} %cot_m.1), channel_id=1, source_target_pairs={{1,0},{0,1},{3,2},{2,3},{5,4},{4,5},{7,6},{6,7},{9,8},{8,9},{11,10... | collective-permute-start | bytes 2752520 | tf_op jit(solution)/shard_map/ppermute | solution.py:17
  1.2 27.7 %collective-permute-start.3 = (bf16[448,1024]{1,0:T(8,128)(2,1)}, bf16[448,1024]{1,0:T(8,128)(2,1)S(1)}, u32[]{:S(2)}, u32[]{:S(2)}) collective-permute-start(bf16[448,1024]{1,0:T(8,128)(2,1)} %tok_m.1), channel_id=1, source_target_pairs={{30,0},{0,2},{2,4},{4,6},{6,8},{8,10},{10,12},{12,14},{14,16},{16,... | collective-permute-start | bytes 2752520 | tf_op jit(solution)/shard_map/ppermute | solution.py:17
  24.0 5.0 %copy-start.10 = (bf16[448,1024]{1,0:T(8,128)(2,1)}, bf16[448,1024]{1,0:T(8,128)(2,1)S(1)}, u32[]{:S(2)}) copy-start(bf16[448,1024]{1,0:T(8,128)(2,1)S(1)} %get-tuple-element.34) | copy-start | bytes 2752516
  28.9 2.6 %copy-start = (bf16[1,2048,384]{2,1,0:T(8,128)(2,1)S(1)}, bf16[1,2048,384]{2,1,0:T(8,128)(2,1)}, u32[]{:S(2)}) copy-start(bf16[1,2048,384]{2,1,0:T(8,128)(2,1)} %param.13) | copy-start | bytes 4718596
  29.0 1.6 %collective-permute-start.4 = (bf16[112,1024]{1,0:T(8,128)(2,1)S(1)}, bf16[112,1024]{1,0:T(8,128)(2,1)S(1)}, u32[]{:S(2)}, u32[]{:S(2)}) collective-permute-start(bf16[112,1024]{1,0:T(8,128)(2,1)S(1)} %get-tuple-element.62), channel_id=1, source_target_pairs={{1,0},{0,1},{3,2},{2,3},{5,4},{4,5},{7,6},{6,7},{9,8},{8,9},{11,10... | collective-permute-start | bytes 688136 | tf_op jit(solution)/shard_map/ppermute | solution.py:17
  29.1 1.8 %collective-permute-start.5 = (bf16[112,1024]{1,0:T(8,128)(2,1)S(1)}, bf16[112,1024]{1,0:T(8,128)(2,1)S(1)}, u32[]{:S(2)}, u32[]{:S(2)}) collective-permute-start(bf16[112,1024]{1,0:T(8,128)(2,1)S(1)} %get-tuple-element.61), channel_id=1, source_target_pairs={{1,0},{0,1},{3,2},{2,3},{5,4},{4,5},{7,6},{6,7},{9,8},{8,9},{11,10... | collective-permute-start | bytes 688136 | tf_op jit(solution)/shard_map/ppermute | solution.py:17
  29.6 26.0 %collective-permute-start.14 = (bf16[448,1024]{1,0:T(8,128)(2,1)S(1)}, bf16[448,1024]{1,0:T(8,128)(2,1)S(1)}, u32[]{:S(2)}, u32[]{:S(2)}) collective-permute-start(bf16[448,1024]{1,0:T(8,128)(2,1)S(1)} %get-tuple-element.35), channel_id=1, source_target_pairs={{30,0},{0,2},{2,4},{4,6},{6,8},{8,10},{10,12},{12,14},{14,16},{16,... | collective-permute-start | bytes 2752520 | tf_op jit(solution)/shard_map/ppermute | solution.py:17
  29.6 1.6 %collective-permute-start.6 = (bf16[112,1024]{1,0:T(8,128)(2,1)S(1)}, bf16[112,1024]{1,0:T(8,128)(2,1)S(1)}, u32[]{:S(2)}, u32[]{:S(2)}) collective-permute-start(bf16[112,1024]{1,0:T(8,128)(2,1)S(1)} %get-tuple-element.60), channel_id=1, source_target_pairs={{1,0},{0,1},{3,2},{2,3},{5,4},{4,5},{7,6},{6,7},{9,8},{8,9},{11,10... | collective-permute-start | bytes 688136 | tf_op jit(solution)/shard_map/ppermute | solution.py:17
  29.7 1.9 %collective-permute-start.7 = (bf16[112,1024]{1,0:T(8,128)(2,1)S(1)}, bf16[112,1024]{1,0:T(8,128)(2,1)S(1)}, u32[]{:S(2)}, u32[]{:S(2)}) collective-permute-start(bf16[112,1024]{1,0:T(8,128)(2,1)S(1)} %get-tuple-element.59), channel_id=1, source_target_pairs={{1,0},{0,1},{3,2},{2,3},{5,4},{4,5},{7,6},{6,7},{9,8},{8,9},{11,10... | collective-permute-start | bytes 688136 | tf_op jit(solution)/shard_map/ppermute | solution.py:17
  31.6 6.6 %copy-start.3 = (bf16[448,1024]{1,0:T(8,128)(2,1)}, bf16[448,1024]{1,0:T(8,128)(2,1)S(1)}, u32[]{:S(2)}) copy-start(bf16[448,1024]{1,0:T(8,128)(2,1)S(1)} %constant_dynamic-update-slice_fusion.tok_o) | copy-start | bytes 2752516
  38.2 1.6 %collective-permute-start.11 = (bf16[112,1024]{1,0:T(8,128)(2,1)S(1)}, bf16[112,1024]{1,0:T(8,128)(2,1)S(1)}, u32[]{:S(2)}, u32[]{:S(2)}) collective-permute-start(bf16[112,1024]{1,0:T(8,128)(2,1)S(1)} %get-tuple-element.56), channel_id=1, source_target_pairs={{1,0},{0,1},{3,2},{2,3},{5,4},{4,5},{7,6},{6,7},{9,8},{8,9},{11,10... | collective-permute-start | bytes 688136 | tf_op jit(solution)/shard_map/ppermute | solution.py:17
  38.5 1.6 %collective-permute-start.10 = (bf16[112,1024]{1,0:T(8,128)(2,1)S(1)}, bf16[112,1024]{1,0:T(8,128)(2,1)S(1)}, u32[]{:S(2)}, u32[]{:S(2)}) collective-permute-start(bf16[112,1024]{1,0:T(8,128)(2,1)S(1)} %get-tuple-element.57), channel_id=1, source_target_pairs={{1,0},{0,1},{3,2},{2,3},{5,4},{4,5},{7,6},{6,7},{9,8},{8,9},{11,10... | collective-permute-start | bytes 688136 | tf_op jit(solution)/shard_map/ppermute | solution.py:17
  38.8 1.6 %collective-permute-start.9 = (bf16[112,1024]{1,0:T(8,128)(2,1)S(1)}, bf16[112,1024]{1,0:T(8,128)(2,1)S(1)}, u32[]{:S(2)}, u32[]{:S(2)}) collective-permute-start(bf16[112,1024]{1,0:T(8,128)(2,1)S(1)} %get-tuple-element.58), channel_id=1, source_target_pairs={{1,0},{0,1},{3,2},{2,3},{5,4},{4,5},{7,6},{6,7},{9,8},{8,9},{11,10... | collective-permute-start | bytes 688136 | tf_op jit(solution)/shard_map/ppermute | solution.py:17
  39.0 1.8 %collective-permute-start.8 = (bf16[112,1024]{1,0:T(8,128)(2,1)S(1)}, bf16[112,1024]{1,0:T(8,128)(2,1)S(1)}, u32[]{:S(2)}, u32[]{:S(2)}) collective-permute-start(bf16[112,1024]{1,0:T(8,128)(2,1)S(1)} %get-tuple-element.55), channel_id=1, source_target_pairs={{1,0},{0,1},{3,2},{2,3},{5,4},{4,5},{7,6},{6,7},{9,8},{8,9},{11,10... | collective-permute-start | bytes 688136 | tf_op jit(solution)/shard_map/ppermute | solution.py:17
  55.7 1.6 %collective-permute-start.15 = (bf16[112,1024]{1,0:T(8,128)(2,1)S(1)}, bf16[112,1024]{1,0:T(8,128)(2,1)S(1)}, u32[]{:S(2)}, u32[]{:S(2)}) collective-permute-start(bf16[112,1024]{1,0:T(8,128)(2,1)S(1)} %get-tuple-element.54), channel_id=1, source_target_pairs={{1,0},{0,1},{3,2},{2,3},{5,4},{4,5},{7,6},{6,7},{9,8},{8,9},{11,10... | collective-permute-start | bytes 688136 | tf_op jit(solution)/shard_map/ppermute | solution.py:17
  55.8 1.8 %collective-permute-start.16 = (bf16[112,1024]{1,0:T(8,128)(2,1)S(1)}, bf16[112,1024]{1,0:T(8,128)(2,1)S(1)}, u32[]{:S(2)}, u32[]{:S(2)}) collective-permute-start(bf16[112,1024]{1,0:T(8,128)(2,1)S(1)} %get-tuple-element.53), channel_id=1, source_target_pairs={{1,0},{0,1},{3,2},{2,3},{5,4},{4,5},{7,6},{6,7},{9,8},{8,9},{11,10... | collective-permute-start | bytes 688136 | tf_op jit(solution)/shard_map/ppermute | solution.py:17
  56.3 16.5 %collective-permute-start.2 = (bf16[448,1024]{1,0:T(8,128)(2,1)}, bf16[448,1024]{1,0:T(8,128)(2,1)}, u32[]{:S(2)}, u32[]{:S(2)}) collective-permute-start(bf16[448,1024]{1,0:T(8,128)(2,1)} %get-tuple-element.29.refs_1_), channel_id=1, source_target_pairs={{1,0},{0,1},{3,2},{2,3},{5,4},{4,5},{7,6},{6,7},{9,8},{8,9},{11,10... | collective-permute-start | bytes 2752520 | tf_op jit(solution)/shard_map/ppermute | solution.py:17
  56.3 23.3 %collective-permute-start.12 = (bf16[448,1024]{1,0:T(8,128)(2,1)S(1)}, bf16[448,1024]{1,0:T(8,128)(2,1)}, u32[]{:S(2)}, u32[]{:S(2)}) collective-permute-start(bf16[448,1024]{1,0:T(8,128)(2,1)S(1)} %add_convert_fusion.3.refs_1_), channel_id=1, source_target_pairs={{2,0},{4,2},{6,4},{8,6},{10,8},{12,10},{14,12},{16,14},{18,16},{20... | collective-permute-start | bytes 2752520 | tf_op jit(solution)/shard_map/ppermute | solution.py:17
  56.3 2.7 %collective-permute-start.17 = (bf16[112,1024]{1,0:T(8,128)(2,1)S(1)}, bf16[112,1024]{1,0:T(8,128)(2,1)S(1)}, u32[]{:S(2)}, u32[]{:S(2)}) collective-permute-start(bf16[112,1024]{1,0:T(8,128)(2,1)S(1)} %get-tuple-element.52), channel_id=1, source_target_pairs={{1,0},{0,1},{3,2},{2,3},{5,4},{4,5},{7,6},{6,7},{9,8},{8,9},{11,10... | collective-permute-start | bytes 688136 | tf_op jit(solution)/shard_map/ppermute | solution.py:17
  57.2 2.3 %collective-permute-start.18 = (bf16[112,1024]{1,0:T(8,128)(2,1)S(1)}, bf16[112,1024]{1,0:T(8,128)(2,1)S(1)}, u32[]{:S(2)}, u32[]{:S(2)}) collective-permute-start(bf16[112,1024]{1,0:T(8,128)(2,1)S(1)} %get-tuple-element.51), channel_id=1, source_target_pairs={{1,0},{0,1},{3,2},{2,3},{5,4},{4,5},{7,6},{6,7},{9,8},{8,9},{11,10... | collective-permute-start | bytes 688136 | tf_op jit(solution)/shard_map/ppermute | solution.py:17
  59.5 7.0 %copy-start.5 = (bf16[448,1024]{1,0:T(8,128)(2,1)}, bf16[448,1024]{1,0:T(8,128)(2,1)S(1)}, u32[]{:S(2)}) copy-start(bf16[448,1024]{1,0:T(8,128)(2,1)S(1)} %constant_dynamic-update-slice_fusion.4.cot_o) | copy-start | bytes 2752516
  67.7 2.2 %collective-permute-start.20 = (bf16[224,1024]{1,0:T(8,128)(2,1)}, bf16[224,1024]{1,0:T(8,128)(2,1)}, u32[]{:S(2)}, u32[]{:S(2)}) collective-permute-start(bf16[224,1024]{1,0:T(8,128)(2,1)} %get-tuple-element.50), channel_id=1, source_target_pairs={{1,0},{0,1},{3,2},{2,3},{5,4},{4,5},{7,6},{6,7},{9,8},{8,9},{11,10... | collective-permute-start | bytes 1376264 | tf_op jit(solution)/shard_map/ppermute | solution.py:17
  67.9 2.6 %collective-permute-start.19 = (bf16[224,1024]{1,0:T(8,128)(2,1)}, bf16[224,1024]{1,0:T(8,128)(2,1)}, u32[]{:S(2)}, u32[]{:S(2)}) collective-permute-start(bf16[224,1024]{1,0:T(8,128)(2,1)} %get-tuple-element.49), channel_id=1, source_target_pairs={{1,0},{0,1},{3,2},{2,3},{5,4},{4,5},{7,6},{6,7},{9,8},{8,9},{11,10... | collective-permute-start | bytes 1376264 | tf_op jit(solution)/shard_map/ppermute | solution.py:17
  68.4 21.4 %collective-permute-start.13 = (bf16[448,1024]{1,0:T(8,128)(2,1)}, bf16[448,1024]{1,0:T(8,128)(2,1)S(1)}, u32[]{:S(2)}, u32[]{:S(2)}) collective-permute-start(bf16[448,1024]{1,0:T(8,128)(2,1)} %copy-done.10), channel_id=1, source_target_pairs={{1,0},{0,1},{3,2},{2,3},{5,4},{4,5},{7,6},{6,7},{9,8},{8,9},{11,10... | collective-permute-start | bytes 2752520 | tf_op jit(solution)/shard_map/ppermute | solution.py:17
  70.5 9.1 %copy-start.17 = (f32[448,1024]{1,0:T(8,128)S(1)}, f32[448,1024]{1,0:T(8,128)}, u32[]{:S(2)}) copy-start(f32[448,1024]{1,0:T(8,128)} %get-tuple-element.28) | copy-start | bytes 5505028
  72.7 26.0 %collective-permute-start.21 = (bf16[448,1024]{1,0:T(8,128)(2,1)S(1)}, bf16[448,1024]{1,0:T(8,128)(2,1)S(1)}, u32[]{:S(2)}, u32[]{:S(2)}) collective-permute-start(bf16[448,1024]{1,0:T(8,128)(2,1)S(1)} %add_convert_fusion.1.rest_0_), channel_id=1, source_target_pairs={{2,0},{4,2},{6,4},{8,6},{10,8},{12,10},{14,12},{16,14},{18,16},{20... | collective-permute-start | bytes 2752520 | tf_op jit(solution)/shard_map/ppermute | solution.py:17
  79.6 2.9 %copy-start.4 = (bf16[448,1024]{1,0:T(8,128)(2,1)S(1)}, bf16[448,1024]{1,0:T(8,128)(2,1)}, u32[]{:S(2)}) copy-start(bf16[448,1024]{1,0:T(8,128)(2,1)} %copy-done.3) | copy-start | bytes 2752516
  79.6 2.9 %copy-start.6 = (bf16[448,1024]{1,0:T(8,128)(2,1)S(1)}, bf16[448,1024]{1,0:T(8,128)(2,1)}, u32[]{:S(2)}) copy-start(bf16[448,1024]{1,0:T(8,128)(2,1)} %copy-done.5) | copy-start | bytes 2752516
  79.6 2.9 %copy-start.12 = (bf16[448,384]{1,0:T(8,128)(2,1)S(1)}, bf16[448,384]{1,0:T(8,128)(2,1)}, u32[]{:S(2)}) copy-start(bf16[448,384]{1,0:T(8,128)(2,1)} %copy-done.11) | copy-start | bytes 1032196
  79.6 2.9 %copy-start.14 = (bf16[448,384]{1,0:T(8,128)(2,1)S(1)}, bf16[448,384]{1,0:T(8,128)(2,1)}, u32[]{:S(2)}) copy-start(bf16[448,384]{1,0:T(8,128)(2,1)} %copy-done.13) | copy-start | bytes 1032196
  82.5 16.2 %copy-start.15 = (f32[448,1024]{1,0:T(8,128)S(1)}, f32[448,1024]{1,0:T(8,128)}, u32[]{:S(2)}) copy-start(f32[448,1024]{1,0:T(8,128)} %get-tuple-element.33) | copy-start | bytes 5505028
  (8 other events, 9.7 us)

commit v2 on v1

--- a/solution.py
+++ b/solution.py
@@ -25,6 +25,17 @@
         passed_along(block[i * step : (i + 1) * step], "dp", 1) for i in range(pieces)
     ]
     return jnp.concatenate(swapped, axis=0)
+
+
+def returned(keep, send, pieces, cuts):
+    step = keep.shape[0] // pieces
+    parts = []
+    for count in cuts:
+        first = len(parts) and sum(part.shape[0] for part in parts)
+        rows = slice(first, first + count * step)
+        other = partner(send[rows], count)
+        parts.append((keep[rows] + other.astype(F32)).astype(BF16))
+    return parts, jnp.concatenate([passed_along(part, "blk", -1) for part in parts], axis=0)
 
 
 def matmul(left_side, right_side):
@@ -55,17 +66,17 @@
     )(*operands)
 
 
-def after(block, ready):
+def after(block, *ready):
     return pl.pallas_call(
         lambda *refs: None,
         out_shape=jax.ShapeDtypeStruct(block.shape, block.dtype),
-        in_specs=[ANY, ANY],
+        in_specs=[ANY] * (1 + len(ready)),
         out_specs=ANY,
         input_output_aliases={0: 0},
         compiler_params=pltpu.CompilerParams(vmem_limit_bytes=2**20),
         cost_estimate=pl.CostEstimate(flops=1, bytes_accessed=1, transcendentals=0),
         name="after",
-    )(block, ready)
+    )(block, *ready)
 
 
 def sides(place, width):
@@ -90,7 +101,9 @@
     gate_own[...] = jnp.sum(own, axis=1, keepdims=True)
     column = jnp.sum(following, axis=1, keepdims=True)
     gate_next[...] = column
-    scaled[...] = (column * cot[...].astype(F32)).astype(BF16)
+    scaled[pl.ds(0, count), :] = (column * cot[...].astype(F32)).astype(BF16)
+    if 0:
+        scaled[pl.ds(count, 0), :] = jnp.zeros((0, cot.shape[1]), BF16)
 
 
 def forward(tok_mine, tok_other, w_first, w_second, mine, other):
@@ -150,8 +163,9 @@
 
 def guest_backward_body(
     place, cot_m, cot_o, w_first, w_second, w_third, active, slope_up,
-    back_send, back_keep, one_ref, two_ref,
-):
+    *rest
+):
+    back_send, back_keep, one_ref, two_ref = rest[-4:]
     mine, other = sides(place, cot_m.shape[1])
     one, two = backward(cot_m[...], cot_o[...], w_third, mine, other, active[...], slope_up[...])
     back_send[...] = back_rows(one, two, w_first, w_second, other).astype(BF16)
@@ -187,7 +201,7 @@
 
     guest_tokens = passed_along(tokens, "blk", 1)
     gate_own, gate_next, scaled_next = call(
-        gates_body, [column, column, rows16], [SMEM, SMEM, VMEM, VMEM, VMEM],
+        gates_body, [column, column, ((tokens.shape[0] + 0, tokens.shape[1]), BF16)], [SMEM, SMEM, VMEM, VMEM, VMEM],
         place, block_expert, block_tokens, block_gate.astype(F32), cotangent,
         name="gates",
     )
@@ -204,7 +218,7 @@
     own_back = back_keep + partner(back_send).astype(F32)
 
     guest_tokens = after(guest_tokens, out_send)
-    guest_other = partner(guest_tokens, 4)
+    guest_other = partner(guest_tokens, 2)
     lent_send, lent_keep, active, slope_up, hidden = call(
         guest_forward_body,
         [rows16, rows, (units, F32), (units, F32), (units, BF16)],
@@ -212,28 +226,26 @@
         place, guest_tokens, guest_other, *weights,
         name="guest_forward",
     )
-    lent_out = (lent_keep + partner(lent_send, 4).astype(F32)).astype(BF16)
-    came_out = passed_along(lent_out, "blk", -1)
-
-    guest_cot = after(guest_cot, lent_out)
-    cot_other = partner(guest_cot, 4)
+    lent_out, came_out = returned(lent_keep, lent_send, 1, (1,))
+
+    guest_cot = after(guest_cot, lent_send)[: tokens.shape[0]]
+    cot_other = partner(guest_cot, 2)
     lent_send, lent_keep, one, two = call(
         guest_backward_body,
         [rows16, rows, (units, BF16), (units, BF16)],
-        [SMEM] + [VMEM] * 7,
-        place, guest_cot, cot_other, *weights, active, slope_up,
-        name="guest_backward",
-    )
-    lent_back = (lent_keep + partner(lent_send, 2).astype(F32)).astype(BF16)
-    came_back = passed_along(lent_back, "blk", -1)
+        [SMEM] + [VMEM] * 7 + [ANY] * len(lent_out),
+        place, guest_cot, cot_other, *weights, active, slope_up, *lent_out,
+        name="guest_backward", flops=1,
+    )
+    lent_back, came_back = returned(lent_keep, lent_send, 4, (4,))
     outputs = (own_out + gate_next * came_out.astype(F32)).astype(BF16)
     grads = call(
         grads_body,
         [(weight.shape, BF16) for weight in (w_gate, w_up, w_down)],
-        [SMEM] + [VMEM] * 10 + [ANY, ANY],
+        [SMEM] + [VMEM] * 10 + [ANY] * (1 + len(lent_back)),
         place, guest_tokens, guest_other, guest_cot, cot_other, hidden, one, two, *own_grads,
-        lent_back, outputs,
-        name="grads", flops=30*10**9,
+        *lent_back, outputs,
+        name="grads", flops=100*10**9,
     )
     backs = own_back + came_back.astype(F32)
     return (outputs, backs.astype(BF16), *grads)

time: 100 us -> 96.3 us (0.963)
  waiting for transfers between devices: 42.6 us -> 35.3 us
  starting transfers between devices: 7.71 us -> 11 us
    ppermute x22 -> x17, waiting for transfers between devices: 42.6 us -> 35.3 us  [passed_along(): lax.ppermute(block, axis, [((i - distance) % size, i) for i in range(size)])]
    ppermute x22 -> x17, starting transfers between devices: 7.71 us -> 11 us  [passed_along(): lax.ppermute(block, axis, [((i - distance) % size, i) for i in range(size)])]
    unnamed x42 -> x38, local copies, waits for them, and re-layouts: 5.12 us -> 5.13 us
  transfers between devices with their start and end apart: 22 -> 17, of which waited for: 18 -> 10; matrix products, arithmetic and copies ran while one was open for 7% -> 8% of each run, Pallas kernels for 35% -> 36%
where the time goes in v2:
time: 96.3 us; the launch traced here: 95.9 us
  waiting for transfers between devices  35.3 us (37%)
  Pallas kernels  34.9 us (36%)
  starting transfers between devices  11 us (11%)
  other arithmetic  7.68 us (8%)
  local copies, waits for them, and re-layouts  6.24 us (6%)
    ppermute x17, waiting for transfers between devices, passed_along(): lax.ppermute(block, axis, [((i - distance) % size, i) for i in range(size)])  35.3 us
    pallas_call x5, Pallas kernels, call(): pl.pallas_call(body, out_shape=[jax.ShapeDtypeStruct(shape, kind) for sha...  34.9 us
    ppermute x17, starting transfers between devices, passed_along(): lax.ppermute(block, axis, [((i - distance) % size, i) for i in range(size)])  11 us
    unnamed x38, local copies, waits for them, and re-layouts  5.13 us
    convert_element_type x1, other arithmetic, on_device(): outputs = (own_out + gate_next * came_out.astype(F32)).astype(BF16)  2.95 us
    convert_element_type x2, other arithmetic, returned(): parts.append((keep[rows] + other.astype(F32)).astype(BF16))  2.44 us
  transfers between devices with their start and end apart: 17, of which 10 were waited for; matrix products, arithmetic and copies ran while one was open for 8% of the time, Pallas kernels for 36%

profile of v2, /device:TPU:0, one launch (start us, length us, event | category | flops | bytes accessed | tf_op | source)
XLA Modules:
  0.0 95.9 jit_solution(6730217336568535514)
XLA Ops:
  0.6 0.5 collective-permute-start
  1.2 2.9 %collective-permute-start.3 = (bf16[448,1024]{1,0:T(8,128)(2,1)}, bf16[448,1024]{1,0:T(8,128)(2,1)S(1)}, u32[]{:S(2)}, u32[]{:S(2)}) collective-permute-start(bf16[448,1024]{1,0:T(8,128)(2,1)} %tok_m.1), channel_id=1, source_target_pairs={{30,0},{0,2},{2,4},{4,6},{6,8},{8,10},{10,12},{12,14},{14,16},{16,... | collective-permute-start | bytes 2752520 | tf_op jit(solution)/shard_map/ppermute | solution.py:17
  4.1 0.7 convert_element_type.33.slot_gate
  4.9 1.2 %copy-done.1 = bf16[448,1024]{1,0:T(8,128)(2,1)S(1)} copy-done((bf16[448,1024]{1,0:T(8,128)(2,1)S(1)}, bf16[448,1024]{1,0:T(8,128)(2,1)}, u32[]{:S(2)}) %copy-start.1) | copy-done | bytes 917528
  6.1 0.7 copy-done.8
  6.8 0.7 copy-done.9
  7.4 1.6 %gates.1 = (f32[448,1]{1,0:T(8,128)S(1)}, f32[448,1]{1,0:T(8,128)S(1)}, bf16[448,1024]{1,0:T(8,128)(2,1)S(1)}) custom-call(s32[3]{0:T(128)S(1)} %pad_add_fusion.place, s32[14]{0:T(128)S(1)} %copy-done.9, s32[14,64]{1,0:T(8,128)S(1)} %copy-done.8, f32[14,64]{1,0:T(8,128)S(1)} %convert_element_type.33.slot_gate, bf16[448,1024]{1,0:T(8,128)(2,1)S(1)} %copy-done.1), custom_call_target="tpu_custom_call" | custom-call | flops 1 | bytes 1 | tf_op jit(solution)/shard_map/gates/pallas_call | solution.py:58
  9.1 1.5 %collective-permute-start.9 = (bf16[448,1024]{1,0:T(8,128)(2,1)S(1)}, bf16[448,1024]{1,0:T(8,128)(2,1)S(1)}, u32[]{:S(2)}, u32[]{:S(2)}) collective-permute-start(bf16[448,1024]{1,0:T(8,128)(2,1)S(1)} %get-tuple-element.35), channel_id=1, source_target_pairs={{30,0},{0,2},{2,4},{4,6},{6,8},{8,10},{10,12},{12,14},{14,16},{16,... | collective-permute-start | bytes 2752520 | tf_op jit(solution)/shard_map/ppermute | solution.py:17
  10.6 1.2 %copy-done.2 = bf16[448,1024]{1,0:T(8,128)(2,1)S(1)} copy-done((bf16[448,1024]{1,0:T(8,128)(2,1)S(1)}, bf16[448,1024]{1,0:T(8,128)(2,1)}, u32[]{:S(2)}) %copy-start.2) | copy-done | bytes 917528
  11.8 1.2 %copy-done.7 = bf16[448,1024]{1,0:T(8,128)(2,1)S(1)} copy-done((bf16[448,1024]{1,0:T(8,128)(2,1)S(1)}, bf16[448,1024]{1,0:T(8,128)(2,1)}, u32[]{:S(2)}) %copy-start.7) | copy-done | bytes 917528
  13.0 12.8 %own.1 = (bf16[448,1024]{1,0:T(8,128)(2,1)}, f32[448,1024]{1,0:T(8,128)}, bf16[448,1024]{1,0:T(8,128)(2,1)S(1)}, f32[448,1024]{1,0:T(8,128)}, bf16[2048,384]{1,0...) custom-call(s32[3]{0:T(128)S(1)} %pad_add_fusion.place, bf16[448,1024]{1,0:T(8,128)(2,1)S(1)} %copy-done.7, ...), custom_call_target="tpu_custom_call" | custom-call | flops 1 | bytes 1 | tf_op jit(solution)/shard_map/own/pallas_call | solution.py:58
  25.8 3.7 %collective-permute-done.3.refs_0_ = bf16[448,1024]{1,0:T(8,128)(2,1)S(1)} collective-permute-done((bf16[448,1024]{1,0:T(8,128)(2,1)}, bf16[448,1024]{1,0:T(8,128)(2,1)S(1)}, u32[]{:S(2)}, u32[]{:S(2)}) %collective-permute-start.3) | collective-permute-done | bytes 917536 | tf_op jit(solution)/shard_map/ppermute | solution.py:17
  29.7 0.5 collective-permute-start.5
  30.1 1.3 %collective-permute-done.4 = bf16[224,1024]{1,0:T(8,128)(2,1)S(1)} collective-permute-done((bf16[224,1024]{1,0:T(8,128)(2,1)S(1)}, bf16[224,1024]{1,0:T(8,128)(2,1)S(1)}, u32[]{:S(2)}, u32[]{:S(2)}) %collective-permute-start.4) | collective-permute-done | bytes 458784 | tf_op jit(solution)/shard_map/ppermute | solution.py:17
  31.5 0.6 collective-permute-done.5
  32.2 6.6 %guest_forward.1 = (bf16[448,1024]{1,0:T(8,128)(2,1)S(1)}, f32[448,1024]{1,0:T(8,128)}, f32[448,384]{1,0:T(8,128)S(1)}, f32[448,384]{1,0:T(8,128)S(1)}, bf16[448,384]{1,0:T(8,128)(2,1)S(1)}) custom-call(s32[3]{0:T(128)S(1)} %pad_add_fusion.place, bf16[448,1024]{1,0:T(8,128)(2,1)S(1)} %after.2.tok_m, ...), custom_call_target="tpu_custom_call" | custom-call | flops 1 | bytes 1 | tf_op jit(solution)/shard_map/guest_forward/pallas_call | solution.py:58
  38.9 9.7 %collective-permute-done.9.refs_0_ = bf16[448,1024]{1,0:T(8,128)(2,1)S(1)} collective-permute-done((bf16[448,1024]{1,0:T(8,128)(2,1)S(1)}, bf16[448,1024]{1,0:T(8,128)(2,1)S(1)}, u32[]{:S(2)}, u32[]{:S(2)}) %collective-permute-start.9) | collective-permute-done | bytes 917536 | tf_op jit(solution)/shard_map/ppermute | solution.py:17
  49.3 1.2 %collective-permute-done.10 = bf16[224,1024]{1,0:T(8,128)(2,1)S(1)} collective-permute-done((bf16[224,1024]{1,0:T(8,128)(2,1)S(1)}, bf16[224,1024]{1,0:T(8,128)(2,1)S(1)}, u32[]{:S(2)}, u32[]{:S(2)}) %collective-permute-start.10) | collective-permute-done | bytes 458784 | tf_op jit(solution)/shard_map/ppermute | solution.py:17
  50.6 1.3 %collective-permute-done.11 = bf16[224,1024]{1,0:T(8,128)(2,1)S(1)} collective-permute-done((bf16[224,1024]{1,0:T(8,128)(2,1)S(1)}, bf16[224,1024]{1,0:T(8,128)(2,1)S(1)}, u32[]{:S(2)}, u32[]{:S(2)}) %collective-permute-start.11) | collective-permute-done | bytes 458784 | tf_op jit(solution)/shard_map/ppermute | solution.py:17
  52.3 2.0 %collective-permute-start.7 = (bf16[448,1024]{1,0:T(8,128)(2,1)S(1)}, bf16[448,1024]{1,0:T(8,128)(2,1)}, u32[]{:S(2)}, u32[]{:S(2)}) collective-permute-start(bf16[448,1024]{1,0:T(8,128)(2,1)S(1)} %add_convert_fusion.3.rest_0_), channel_id=1, source_target_pairs={{2,0},{4,2},{6,4},{8,6},{10,8},{12,10},{14,12},{16,14},{18,16},{20... | collective-permute-start | bytes 2752520 | tf_op jit(solution)/shard_map/ppermute | solution.py:17
  54.2 6.7 %guest_backward.1 = (bf16[448,1024]{1,0:T(8,128)(2,1)S(1)}, f32[448,1024]{1,0:T(8,128)}, bf16[448,384]{1,0:T(8,128)(2,1)S(1)}, bf16[448,384]{1,0:T(8,128)(2,1)S(1)}) custom-call(s32[3]{0:T(128)S(1)} %pad_add_fusion.place, bf16[448,1024]{1,0:T(8,128)(2,1)S(1)} %after.3.cot_m, bf16[448,1024]{1,0:T(8,128)(2,1)S(1)} %constant_dynamic-update-slice_fusion.2.cot_o, ...), custom_call_target="tpu_custom_call" | custom-call | flops 1 | bytes 1 | tf_op jit(solution)/shard_map/guest_backward/pallas_call | solution.py:58
  60.9 0.9 fusion
  62.0 0.5 collective-permute-start.14
  62.5 1.4 %collective-permute-done.15 = bf16[112,1024]{1,0:T(8,128)(2,1)} collective-permute-done((bf16[112,1024]{1,0:T(8,128)(2,1)S(1)}, bf16[112,1024]{1,0:T(8,128)(2,1)}, u32[]{:S(2)}, u32[]{:S(2)}) %collective-permute-start.15) | collective-permute-done | bytes 229408 | tf_op jit(solution)/shard_map/ppermute | solution.py:17
  64.6 1.1 %collective-permute-done.12 = bf16[112,1024]{1,0:T(8,128)(2,1)} collective-permute-done((bf16[112,1024]{1,0:T(8,128)(2,1)}, bf16[112,1024]{1,0:T(8,128)(2,1)}, u32[]{:S(2)}, u32[]{:S(2)}) %collective-permute-start.12) | collective-permute-done | bytes 229408 | tf_op jit(solution)/shard_map/ppermute | solution.py:17
  65.7 2.1 %add_convert_fusion.1.rest_0_ = bf16[448,1024]{1,0:T(8,128)(2,1)S(1)} fusion(f32[448,1024]{1,0:T(8,128)} %get-tuple-element.38, bf16[112,1024]{1,0:T(8,128)(2,1)} %collective-permute-done.15, bf16[112,1024]{1,0:T(8,128)(2,1)} %collective-permute-done.14, bf16[112,1024]{1,0:T(8,128)(2,1)} %collective-permute-done.13, bf16[112,1024]{1,0:T(8,128)(2,1)} %collective-permute-done.12), kind=kLoop, calls=%fused_computation.1 | loop fusion | flops 4587520 | bytes 3670016 | tf_op jit(solution)/shard_map/convert_element_type | solution.py:37
  67.9 1.5 %collective-permute-start.16 = (bf16[448,1024]{1,0:T(8,128)(2,1)S(1)}, bf16[448,1024]{1,0:T(8,128)(2,1)S(1)}, u32[]{:S(2)}, u32[]{:S(2)}) collective-permute-start(bf16[448,1024]{1,0:T(8,128)(2,1)S(1)} %add_convert_fusion.1.rest_0_), channel_id=1, source_target_pairs={{2,0},{4,2},{6,4},{8,6},{10,8},{12,10},{14,12},{16,14},{18,16},{20... | collective-permute-start | bytes 2752520 | tf_op jit(solution)/shard_map/ppermute | solution.py:17
  69.4 6.4 %collective-permute-done.7 = bf16[448,1024]{1,0:T(8,128)(2,1)} collective-permute-done((bf16[448,1024]{1,0:T(8,128)(2,1)S(1)}, bf16[448,1024]{1,0:T(8,128)(2,1)}, u32[]{:S(2)}, u32[]{:S(2)}) %collective-permute-start.7) | collective-permute-done | bytes 917536 | tf_op jit(solution)/shard_map/ppermute | solution.py:17
  75.8 2.9 %add_convert_fusion.2.rest_1_ = bf16[448,1024]{1,0:T(8,128)(2,1)} fusion(bf16[448,1024]{1,0:T(8,128)(2,1)} %collective-permute-done.7, f32[448,1024]{1,0:T(8,128)S(1)} %copy-done.17, bf16[448,1024]{1,0:T(8,128)(2,1)} %collective-permute-done.2, f32[448]{0:T(512)S(1)} %reduce), kind=kLoop, calls=%fused_computation.2 | loop fusion | flops 2752512 | bytes 4589312 | tf_op jit(solution)/shard_map/convert_element_type | solution.py:241
  78.8 7.2 %grads.1 = (bf16[1,2048,384]{2,1,0:T(8,128)(2,1)}, bf16[1,2048,384]{2,1,0:T(8,128)(2,1)}, bf16[1,384,2048]{2,1,0:T(8,128)(2,1)}) custom-call(s32[3]{0:T(128)S(1)} %pad_add_fusion.place, bf16[448,1024]{1,0:T(8,128)(2,1)S(1)} %after.2.tok_m, bf16[448,1024]{1,0:T(8,128)(2,1)S(1)} %copy-done.6, bf16[448,1024]{1,0:T(8,128)(2,1)S(1)} %after.3.cot_m, ...), custom_call_target="tpu_custom_call" | custom-call | flops 99999997952 | bytes 1 | tf_op jit(solution)/shard_map/grads/pallas_call | solution.py:58
  86.0 8.5 %collective-permute-done.16 = bf16[448,1024]{1,0:T(8,128)(2,1)S(1)} collective-permute-done((bf16[448,1024]{1,0:T(8,128)(2,1)S(1)}, bf16[448,1024]{1,0:T(8,128)(2,1)S(1)}, u32[]{:S(2)}, u32[]{:S(2)}) %collective-permute-start.16) | collective-permute-done | bytes 917536 | tf_op jit(solution)/shard_map/ppermute | solution.py:17
  94.5 1.4 %add_convert_fusion = bf16[448,1024]{1,0:T(8,128)(2,1)} fusion(bf16[448,1024]{1,0:T(8,128)(2,1)S(1)} %collective-permute-done.16, f32[448,1024]{1,0:T(8,128)S(1)} %copy-done.15, bf16[448,1024]{1,0:T(8,128)(2,1)S(1)} %collective-permute-done.8), kind=kLoop, calls=%fused_computation | loop fusion | flops 2293760 | bytes 4587520 | tf_op jit(solution)/shard_map/convert_element_type | solution.py:251
  (59 shorter events, 2.5 us)
Async XLA Ops:
  0.6 10.0 %collective-permute-start = (bf16[448,1024]{1,0:T(8,128)(2,1)}, bf16[448,1024]{1,0:T(8,128)(2,1)S(1)}, u32[]{:S(2)}, u32[]{:S(2)}) collective-permute-start(bf16[448,1024]{1,0:T(8,128)(2,1)} %tok_m.1), channel_id=1, source_target_pairs={{1,0},{0,1},{3,2},{2,3},{5,4},{4,5},{7,6},{6,7},{9,8},{8,9},{11,10... | collective-permute-start | bytes 2752520 | tf_op jit(solution)/shard_map/ppermute | solution.py:17
  1.1 9.5 %collective-permute-start.1 = (bf16[448,1024]{1,0:T(8,128)(2,1)}, bf16[448,1024]{1,0:T(8,128)(2,1)}, u32[]{:S(2)}, u32[]{:S(2)}) collective-permute-start(bf16[448,1024]{1,0:T(8,128)(2,1)} %cot_m.1), channel_id=1, source_target_pairs={{1,0},{0,1},{3,2},{2,3},{5,4},{4,5},{7,6},{6,7},{9,8},{8,9},{11,10... | collective-permute-start | bytes 2752520 | tf_op jit(solution)/shard_map/ppermute | solution.py:17
  1.2 28.3 %collective-permute-start.3 = (bf16[448,1024]{1,0:T(8,128)(2,1)}, bf16[448,1024]{1,0:T(8,128)(2,1)S(1)}, u32[]{:S(2)}, u32[]{:S(2)}) collective-permute-start(bf16[448,1024]{1,0:T(8,128)(2,1)} %tok_m.1), channel_id=1, source_target_pairs={{30,0},{0,2},{2,4},{4,6},{6,8},{8,10},{10,12},{12,14},{14,16},{16,... | collective-permute-start | bytes 2752520 | tf_op jit(solution)/shard_map/ppermute | solution.py:17
  4.9 1.2 %copy-start.1 = (bf16[448,1024]{1,0:T(8,128)(2,1)S(1)}, bf16[448,1024]{1,0:T(8,128)(2,1)}, u32[]{:S(2)}) copy-start(bf16[448,1024]{1,0:T(8,128)(2,1)} %cot_m.1) | copy-start | bytes 2752516
  9.1 39.5 %collective-permute-start.9 = (bf16[448,1024]{1,0:T(8,128)(2,1)S(1)}, bf16[448,1024]{1,0:T(8,128)(2,1)S(1)}, u32[]{:S(2)}, u32[]{:S(2)}) collective-permute-start(bf16[448,1024]{1,0:T(8,128)(2,1)S(1)} %get-tuple-element.35), channel_id=1, source_target_pairs={{30,0},{0,2},{2,4},{4,6},{6,8},{8,10},{10,12},{12,14},{14,16},{16,... | collective-permute-start | bytes 2752520 | tf_op jit(solution)/shard_map/ppermute | solution.py:17
  10.6 1.2 %copy-start.2 = (bf16[448,1024]{1,0:T(8,128)(2,1)S(1)}, bf16[448,1024]{1,0:T(8,128)(2,1)}, u32[]{:S(2)}) copy-start(bf16[448,1024]{1,0:T(8,128)(2,1)} %cot_m.1) | copy-start | bytes 2752516
  11.8 1.2 %copy-start.7 = (bf16[448,1024]{1,0:T(8,128)(2,1)S(1)}, bf16[448,1024]{1,0:T(8,128)(2,1)}, u32[]{:S(2)}) copy-start(bf16[448,1024]{1,0:T(8,128)(2,1)} %tok_m.1) | copy-start | bytes 2752516
  25.8 3.8 %copy-start.10 = (bf16[448,1024]{1,0:T(8,128)(2,1)}, bf16[448,1024]{1,0:T(8,128)(2,1)S(1)}, u32[]{:S(2)}) copy-start(bf16[448,1024]{1,0:T(8,128)(2,1)S(1)} %get-tuple-element.34) | copy-start | bytes 2752516
  29.5 2.7 %copy-start = (bf16[1,2048,384]{2,1,0:T(8,128)(2,1)S(1)}, bf16[1,2048,384]{2,1,0:T(8,128)(2,1)}, u32[]{:S(2)}) copy-start(bf16[1,2048,384]{2,1,0:T(8,128)(2,1)} %param.13) | copy-start | bytes 4718596
  29.6 1.9 %collective-permute-start.4 = (bf16[224,1024]{1,0:T(8,128)(2,1)S(1)}, bf16[224,1024]{1,0:T(8,128)(2,1)S(1)}, u32[]{:S(2)}, u32[]{:S(2)}) collective-permute-start(bf16[224,1024]{1,0:T(8,128)(2,1)S(1)} %get-tuple-element.56), channel_id=1, source_target_pairs={{1,0},{0,1},{3,2},{2,3},{5,4},{4,5},{7,6},{6,7},{9,8},{8,9},{11,10... | collective-permute-start | bytes 1376264 | tf_op jit(solution)/shard_map/ppermute | solution.py:17
  29.7 2.5 %collective-permute-start.5 = (bf16[224,1024]{1,0:T(8,128)(2,1)S(1)}, bf16[224,1024]{1,0:T(8,128)(2,1)S(1)}, u32[]{:S(2)}, u32[]{:S(2)}) collective-permute-start(bf16[224,1024]{1,0:T(8,128)(2,1)S(1)} %get-tuple-element.55), channel_id=1, source_target_pairs={{1,0},{0,1},{3,2},{2,3},{5,4},{4,5},{7,6},{6,7},{9,8},{8,9},{11,10... | collective-permute-start | bytes 1376264 | tf_op jit(solution)/shard_map/ppermute | solution.py:17
  32.2 6.6 %copy-start.5 = (bf16[448,1024]{1,0:T(8,128)(2,1)}, bf16[448,1024]{1,0:T(8,128)(2,1)S(1)}, u32[]{:S(2)}) copy-start(bf16[448,1024]{1,0:T(8,128)(2,1)S(1)} %constant_dynamic-update-slice_fusion.tok_o) | copy-start | bytes 2752516
  38.8 13.1 %collective-permute-start.6 = (bf16[448,1024]{1,0:T(8,128)(2,1)S(1)}, bf16[448,1024]{1,0:T(8,128)(2,1)S(1)}, u32[]{:S(2)}, u32[]{:S(2)}) collective-permute-start(bf16[448,1024]{1,0:T(8,128)(2,1)S(1)} %get-tuple-element.32.refs_1_), channel_id=1, source_target_pairs={{1,0},{0,1},{3,2},{2,3},{5,4},{4,5},{7,6},{6,7},{9,8},{8,9},{11,10... | collective-permute-start | bytes 2752520 | tf_op jit(solution)/shard_map/ppermute | solution.py:17
  48.6 3.3 %copy-start.16 = (f32[448,1024]{1,0:T(8,128)S(1)}, f32[448,1024]{1,0:T(8,128)}, u32[]{:S(2)}) copy-start(f32[448,1024]{1,0:T(8,128)} %get-tuple-element.31) | copy-start | bytes 5505028
  48.7 1.9 %collective-permute-start.10 = (bf16[224,1024]{1,0:T(8,128)(2,1)S(1)}, bf16[224,1024]{1,0:T(8,128)(2,1)S(1)}, u32[]{:S(2)}, u32[]{:S(2)}) collective-permute-start(bf16[224,1024]{1,0:T(8,128)(2,1)S(1)} %get-tuple-element.54), channel_id=1, source_target_pairs={{1,0},{0,1},{3,2},{2,3},{5,4},{4,5},{7,6},{6,7},{9,8},{8,9},{11,10... | collective-permute-start | bytes 1376264 | tf_op jit(solution)/shard_map/ppermute | solution.py:17
  48.8 3.1 %collective-permute-start.11 = (bf16[224,1024]{1,0:T(8,128)(2,1)S(1)}, bf16[224,1024]{1,0:T(8,128)(2,1)S(1)}, u32[]{:S(2)}, u32[]{:S(2)}) collective-permute-start(bf16[224,1024]{1,0:T(8,128)(2,1)S(1)} %get-tuple-element.53), channel_id=1, source_target_pairs={{1,0},{0,1},{3,2},{2,3},{5,4},{4,5},{7,6},{6,7},{9,8},{8,9},{11,10... | collective-permute-start | bytes 1376264 | tf_op jit(solution)/shard_map/ppermute | solution.py:17
  49.2 20.1 %collective-permute-start.2 = (bf16[448,1024]{1,0:T(8,128)(2,1)}, bf16[448,1024]{1,0:T(8,128)(2,1)}, u32[]{:S(2)}, u32[]{:S(2)}) collective-permute-start(bf16[448,1024]{1,0:T(8,128)(2,1)} %get-tuple-element.29.refs_1_), channel_id=1, source_target_pairs={{1,0},{0,1},{3,2},{2,3},{5,4},{4,5},{7,6},{6,7},{9,8},{8,9},{11,10... | collective-permute-start | bytes 2752520 | tf_op jit(solution)/shard_map/ppermute | solution.py:17
  51.9 2.3 %copy-start.3 = (bf16[448,1024]{1,0:T(8,128)(2,1)}, bf16[448,1024]{1,0:T(8,128)(2,1)S(1)}, u32[]{:S(2)}) copy-start(bf16[448,1024]{1,0:T(8,128)(2,1)S(1)} %constant_dynamic-update-slice_fusion.2.cot_o) | copy-start | bytes 2752516
  52.3 23.5 %collective-permute-start.7 = (bf16[448,1024]{1,0:T(8,128)(2,1)S(1)}, bf16[448,1024]{1,0:T(8,128)(2,1)}, u32[]{:S(2)}, u32[]{:S(2)}) collective-permute-start(bf16[448,1024]{1,0:T(8,128)(2,1)S(1)} %add_convert_fusion.3.rest_0_), channel_id=1, source_target_pairs={{2,0},{4,2},{6,4},{8,6},{10,8},{12,10},{14,12},{16,14},{18,16},{20... | collective-permute-start | bytes 2752520 | tf_op jit(solution)/shard_map/ppermute | solution.py:17
  60.9 1.1 %copy-start.13 = (bf16[448,384]{1,0:T(8,128)(2,1)}, bf16[448,384]{1,0:T(8,128)(2,1)S(1)}, u32[]{:S(2)}) copy-start(bf16[448,384]{1,0:T(8,128)(2,1)S(1)} %get-tuple-element.42.two) | copy-start | bytes 1032196
  62.0 1.9 %collective-permute-start.15 = (bf16[112,1024]{1,0:T(8,128)(2,1)S(1)}, bf16[112,1024]{1,0:T(8,128)(2,1)}, u32[]{:S(2)}, u32[]{:S(2)}) collective-permute-start(bf16[112,1024]{1,0:T(8,128)(2,1)S(1)} %get-tuple-element.50), channel_id=1, source_target_pairs={{1,0},{0,1},{3,2},{2,3},{5,4},{4,5},{7,6},{6,7},{9,8},{8,9},{11,10... | collective-permute-start | bytes 688136 | tf_op jit(solution)/shard_map/ppermute | solution.py:17
  62.0 2.2 %collective-permute-start.14 = (bf16[112,1024]{1,0:T(8,128)(2,1)}, bf16[112,1024]{1,0:T(8,128)(2,1)}, u32[]{:S(2)}, u32[]{:S(2)}) collective-permute-start(bf16[112,1024]{1,0:T(8,128)(2,1)} %get-tuple-element.51), channel_id=1, source_target_pairs={{1,0},{0,1},{3,2},{2,3},{5,4},{4,5},{7,6},{6,7},{9,8},{8,9},{11,10... | collective-permute-start | bytes 688136 | tf_op jit(solution)/shard_map/ppermute | solution.py:17
  62.5 2.1 %collective-permute-start.13 = (bf16[112,1024]{1,0:T(8,128)(2,1)}, bf16[112,1024]{1,0:T(8,128)(2,1)}, u32[]{:S(2)}, u32[]{:S(2)}) collective-permute-start(bf16[112,1024]{1,0:T(8,128)(2,1)} %get-tuple-element.52), channel_id=1, source_target_pairs={{1,0},{0,1},{3,2},{2,3},{5,4},{4,5},{7,6},{6,7},{9,8},{8,9},{11,10... | collective-permute-start | bytes 688136 | tf_op jit(solution)/shard_map/ppermute | solution.py:17
  63.9 1.8 %collective-permute-start.12 = (bf16[112,1024]{1,0:T(8,128)(2,1)}, bf16[112,1024]{1,0:T(8,128)(2,1)}, u32[]{:S(2)}, u32[]{:S(2)}) collective-permute-start(bf16[112,1024]{1,0:T(8,128)(2,1)} %get-tuple-element.49), channel_id=1, source_target_pairs={{1,0},{0,1},{3,2},{2,3},{5,4},{4,5},{7,6},{6,7},{9,8},{8,9},{11,10... | collective-permute-start | bytes 688136 | tf_op jit(solution)/shard_map/ppermute | solution.py:17
  64.2 21.8 %collective-permute-start.8 = (bf16[448,1024]{1,0:T(8,128)(2,1)}, bf16[448,1024]{1,0:T(8,128)(2,1)S(1)}, u32[]{:S(2)}, u32[]{:S(2)}) collective-permute-start(bf16[448,1024]{1,0:T(8,128)(2,1)} %copy-done.10), channel_id=1, source_target_pairs={{1,0},{0,1},{3,2},{2,3},{5,4},{4,5},{7,6},{6,7},{9,8},{8,9},{11,10... | collective-permute-start | bytes 2752520 | tf_op jit(solution)/shard_map/ppermute | solution.py:17
  65.7 10.1 %copy-start.17 = (f32[448,1024]{1,0:T(8,128)S(1)}, f32[448,1024]{1,0:T(8,128)}, u32[]{:S(2)}) copy-start(f32[448,1024]{1,0:T(8,128)} %get-tuple-element.28) | copy-start | bytes 5505028
  67.9 26.7 %collective-permute-start.16 = (bf16[448,1024]{1,0:T(8,128)(2,1)S(1)}, bf16[448,1024]{1,0:T(8,128)(2,1)S(1)}, u32[]{:S(2)}, u32[]{:S(2)}) collective-permute-start(bf16[448,1024]{1,0:T(8,128)(2,1)S(1)} %add_convert_fusion.1.rest_0_), channel_id=1, source_target_pairs={{2,0},{4,2},{6,4},{8,6},{10,8},{12,10},{14,12},{16,14},{18,16},{20... | collective-permute-start | bytes 2752520 | tf_op jit(solution)/shard_map/ppermute | solution.py:17
  75.8 3.0 %copy-start.4 = (bf16[448,1024]{1,0:T(8,128)(2,1)S(1)}, bf16[448,1024]{1,0:T(8,128)(2,1)}, u32[]{:S(2)}) copy-start(bf16[448,1024]{1,0:T(8,128)(2,1)} %copy-done.3) | copy-start | bytes 2752516
  75.8 3.0 %copy-start.6 = (bf16[448,1024]{1,0:T(8,128)(2,1)S(1)}, bf16[448,1024]{1,0:T(8,128)(2,1)}, u32[]{:S(2)}) copy-start(bf16[448,1024]{1,0:T(8,128)(2,1)} %copy-done.5) | copy-start | bytes 2752516
  75.8 3.0 %copy-start.12 = (bf16[448,384]{1,0:T(8,128)(2,1)S(1)}, bf16[448,384]{1,0:T(8,128)(2,1)}, u32[]{:S(2)}) copy-start(bf16[448,384]{1,0:T(8,128)(2,1)} %copy-done.11) | copy-start | bytes 1032196
  75.8 3.0 %copy-start.14 = (bf16[448,384]{1,0:T(8,128)(2,1)S(1)}, bf16[448,384]{1,0:T(8,128)(2,1)}, u32[]{:S(2)}) copy-start(bf16[448,384]{1,0:T(8,128)(2,1)} %copy-done.13) | copy-start | bytes 1032196
  78.8 15.8 %copy-start.15 = (f32[448,1024]{1,0:T(8,128)S(1)}, f32[448,1024]{1,0:T(8,128)}, u32[]{:S(2)}) copy-start(f32[448,1024]{1,0:T(8,128)} %get-tuple-element.33) | copy-start | bytes 5505028
  (3 other events, 2.3 us)

commit v3 on v2

--- a/solution.py
+++ b/solution.py
@@ -211,7 +211,7 @@
         own_body,
         [rows16, rows, rows16, rows] + [(weight.shape, BF16) for weight in weights],
         [SMEM] + [VMEM] * 8,
-        place, tokens, partner(tokens), cotangent, partner(cotangent), gate_own, *weights,
+        place, tokens, partner(tokens, 2), cotangent, partner(cotangent, 2), gate_own, *weights,
         name="own",
     )
     own_out = out_keep + partner(out_send).astype(F32)

time: 96.3 us -> 95.4 us (level)
  local copies, waits for them, and re-layouts: 6.24 us -> 4.34 us
  other arithmetic: 7.68 us -> 9.35 us
    unnamed x38, local copies, waits for them, and re-layouts: 5.13 us -> 0.29 us
    slice x3 -> x5, local copies, waits for them, and re-layouts: 1.05 us -> 4 us  [partner(): block[i * step:(i + 1) * step]]
    concatenate x0 -> x2, other arithmetic: none -> 2.36 us  [partner(): return jnp.concatenate(swapped, axis=0)]
    ppermute x17 -> x19, waiting for transfers between devices: 35.3 us -> 34.5 us  [passed_along(): lax.ppermute(block, axis, [((i - distance) % size, i) for i in range(size)])]
    ppermute x17 -> x19, starting transfers between devices: 11 us -> 11.5 us  [passed_along(): lax.ppermute(block, axis, [((i - distance) % size, i) for i in range(size)])]
  transfers between devices with their start and end apart: 17 -> 19, of which waited for: 10 -> 10; matrix products, arithmetic and copies ran while one was open for 8% -> 13% of each run, Pallas kernels for 36% -> 36%
where the time goes in v3:
time: 95.4 us; the launch traced here: 95.2 us
  Pallas kernels  34.7 us (36%)
  waiting for transfers between devices  34.5 us (36%)
  starting transfers between devices  11.5 us (12%)
  other arithmetic  9.35 us (10%)
  local copies, waits for them, and re-layouts  4.34 us (5%)
    pallas_call x5, Pallas kernels, call(): pl.pallas_call(body, out_shape=[jax.ShapeDtypeStruct(shape, kind) for sha...  34.7 us
    ppermute x19, waiting for transfers between devices, passed_along(): lax.ppermute(block, axis, [((i - distance) % size, i) for i in range(size)])  34.5 us
    ppermute x19, starting transfers between devices, passed_along(): lax.ppermute(block, axis, [((i - distance) % size, i) for i in range(size)])  11.5 us
    slice x5, local copies, waits for them, and re-layouts, partner(): block[i * step:(i + 1) * step]  4 us
    convert_element_type x1, other arithmetic, on_device(): outputs = (own_out + gate_next * came_out.astype(F32)).astype(BF16)  2.95 us
    convert_element_type x2, other arithmetic, returned(): parts.append((keep[rows] + other.astype(F32)).astype(BF16))  2.44 us
    concatenate x2, other arithmetic, partner(): return jnp.concatenate(swapped, axis=0)  2.36 us
  transfers between devices with their start and end apart: 19, of which 10 were waited for; matrix products, arithmetic and copies ran while one was open for 13% of the time, Pallas kernels for 36%

profile of v3, /device:TPU:0, one launch (start us, length us, event | category | flops | bytes accessed | tf_op | source)
XLA Modules:
  0.0 95.2 jit_solution(3901822432950210217)
XLA Ops:
  0.7 3.0 %collective-permute-start.5 = (bf16[448,1024]{1,0:T(8,128)(2,1)}, bf16[448,1024]{1,0:T(8,128)(2,1)S(1)}, u32[]{:S(2)}, u32[]{:S(2)}) collective-permute-start(bf16[448,1024]{1,0:T(8,128)(2,1)} %tok_m.1), channel_id=1, source_target_pairs={{30,0},{0,2},{2,4},{4,6},{6,8},{8,10},{10,12},{12,14},{14,16},{16,... | collective-permute-start | bytes 2752520 | tf_op jit(solution)/shard_map/ppermute | solution.py:17
  3.7 2.0 %fusion.4 = (bf16[224,1024]{1,0:T(8,128)(2,1)}, bf16[224,1024]{1,0:T(8,128)(2,1)S(1)}) fusion(bf16[448,1024]{1,0:T(8,128)(2,1)} %tok_m.1), kind=kLoop, calls=%fused_computation.15 | loop fusion | bytes 1835008 | tf_op jit(solution)/shard_map/slice | solution.py:25
  5.7 0.5 collective-permute-start
  6.2 1.0 %fusion.3 = (bf16[224,1024]{1,0:T(8,128)(2,1)}, bf16[224,1024]{1,0:T(8,128)(2,1)}) fusion(bf16[448,1024]{1,0:T(8,128)(2,1)S(1)} %copy-done.1), kind=kLoop, calls=%fused_computation.14 | loop fusion | bytes 1835008 | tf_op jit(solution)/shard_map/slice | solution.py:25
  7.1 0.5 collective-permute-start.2
  7.7 1.6 %gates.1 = (f32[448,1]{1,0:T(8,128)S(1)}, f32[448,1]{1,0:T(8,128)S(1)}, bf16[448,1024]{1,0:T(8,128)(2,1)S(1)}) custom-call(s32[3]{0:T(128)S(1)} %pad_add_fusion.place, s32[14]{0:T(128)S(1)} %copy-done.8, s32[14,64]{1,0:T(8,128)S(1)} %copy-done.7, f32[14,64]{1,0:T(8,128)S(1)} %convert_element_type.33.slot_gate, bf16[448,1024]{1,0:T(8,128)(2,1)S(1)} %copy-done.1), custom_call_target="tpu_custom_call" | custom-call | flops 1 | bytes 1 | tf_op jit(solution)/shard_map/gates/pallas_call | solution.py:58
  9.4 1.5 %collective-permute-start.11 = (bf16[448,1024]{1,0:T(8,128)(2,1)S(1)}, bf16[448,1024]{1,0:T(8,128)(2,1)S(1)}, u32[]{:S(2)}, u32[]{:S(2)}) collective-permute-start(bf16[448,1024]{1,0:T(8,128)(2,1)S(1)} %get-tuple-element.35), channel_id=1, source_target_pairs={{30,0},{0,2},{2,4},{4,6},{6,8},{8,10},{10,12},{12,14},{14,16},{16,... | collective-permute-start | bytes 2752520 | tf_op jit(solution)/shard_map/ppermute | solution.py:17
  10.9 1.1 %pad_maximum_fusion.tok_o = bf16[448,1024]{1,0:T(8,128)(2,1)S(1)} fusion(bf16[224,1024]{1,0:T(8,128)(2,1)S(1)} %collective-permute-done.1, bf16[224,1024]{1,0:T(8,128)(2,1)} %collective-permute-done), kind=kLoop, calls=%fused_computation.4 | loop fusion | flops 1835008 | bytes 1835008 | tf_op jit(solution)/shard_map/concatenate | solution.py:27
  12.1 1.2 %pad_maximum_fusion.1.cot_o = bf16[448,1024]{1,0:T(8,128)(2,1)S(1)} fusion(bf16[224,1024]{1,0:T(8,128)(2,1)} %collective-permute-done.3, bf16[224,1024]{1,0:T(8,128)(2,1)} %collective-permute-done.2), kind=kLoop, calls=%fused_computation.5 | loop fusion | flops 1835008 | bytes 1835008 | tf_op jit(solution)/shard_map/concatenate | solution.py:27
  13.3 12.6 %own.1 = (bf16[448,1024]{1,0:T(8,128)(2,1)}, f32[448,1024]{1,0:T(8,128)}, bf16[448,1024]{1,0:T(8,128)(2,1)S(1)}, f32[448,1024]{1,0:T(8,128)}, bf16[2048,384]{1,0...) custom-call(s32[3]{0:T(128)S(1)} %pad_add_fusion.place, bf16[448,1024]{1,0:T(8,128)(2,1)S(1)} %copy-done.2, ...), custom_call_target="tpu_custom_call" | custom-call | flops 1 | bytes 1 | tf_op jit(solution)/shard_map/own/pallas_call | solution.py:58
  25.9 3.2 %collective-permute-done.5.refs_0_ = bf16[448,1024]{1,0:T(8,128)(2,1)S(1)} collective-permute-done((bf16[448,1024]{1,0:T(8,128)(2,1)}, bf16[448,1024]{1,0:T(8,128)(2,1)S(1)}, u32[]{:S(2)}, u32[]{:S(2)}) %collective-permute-start.5) | collective-permute-done | bytes 917536 | tf_op jit(solution)/shard_map/ppermute | solution.py:17
  29.2 0.5 collective-permute-start.7
  29.7 1.3 %collective-permute-done.6 = bf16[224,1024]{1,0:T(8,128)(2,1)S(1)} collective-permute-done((bf16[224,1024]{1,0:T(8,128)(2,1)S(1)}, bf16[224,1024]{1,0:T(8,128)(2,1)S(1)}, u32[]{:S(2)}, u32[]{:S(2)}) %collective-permute-start.6) | collective-permute-done | bytes 458784 | tf_op jit(solution)/shard_map/ppermute | solution.py:17
  31.0 0.6 collective-permute-done.7
  31.7 6.6 %guest_forward.1 = (bf16[448,1024]{1,0:T(8,128)(2,1)S(1)}, f32[448,1024]{1,0:T(8,128)}, f32[448,384]{1,0:T(8,128)S(1)}, f32[448,384]{1,0:T(8,128)S(1)}, bf16[448,384]{1,0:T(8,128)(2,1)S(1)}) custom-call(s32[3]{0:T(128)S(1)} %pad_add_fusion.place, bf16[448,1024]{1,0:T(8,128)(2,1)S(1)} %after.2.tok_m, ...), custom_call_target="tpu_custom_call" | custom-call | flops 1 | bytes 1 | tf_op jit(solution)/shard_map/guest_forward/pallas_call | solution.py:58
  38.5 9.4 %collective-permute-done.11.refs_0_ = bf16[448,1024]{1,0:T(8,128)(2,1)S(1)} collective-permute-done((bf16[448,1024]{1,0:T(8,128)(2,1)S(1)}, bf16[448,1024]{1,0:T(8,128)(2,1)S(1)}, u32[]{:S(2)}, u32[]{:S(2)}) %collective-permute-start.11) | collective-permute-done | bytes 917536 | tf_op jit(solution)/shard_map/ppermute | solution.py:17
  48.0 0.5 collective-permute-start.13
  48.6 1.2 %collective-permute-done.12 = bf16[224,1024]{1,0:T(8,128)(2,1)S(1)} collective-permute-done((bf16[224,1024]{1,0:T(8,128)(2,1)S(1)}, bf16[224,1024]{1,0:T(8,128)(2,1)S(1)}, u32[]{:S(2)}, u32[]{:S(2)}) %collective-permute-start.12) | collective-permute-done | bytes 458784 | tf_op jit(solution)/shard_map/ppermute | solution.py:17
  49.9 1.3 %collective-permute-done.13 = bf16[224,1024]{1,0:T(8,128)(2,1)S(1)} collective-permute-done((bf16[224,1024]{1,0:T(8,128)(2,1)S(1)}, bf16[224,1024]{1,0:T(8,128)(2,1)S(1)}, u32[]{:S(2)}, u32[]{:S(2)}) %collective-permute-start.13) | collective-permute-done | bytes 458784 | tf_op jit(solution)/shard_map/ppermute | solution.py:17
  51.5 2.0 %collective-permute-start.9 = (bf16[448,1024]{1,0:T(8,128)(2,1)S(1)}, bf16[448,1024]{1,0:T(8,128)(2,1)}, u32[]{:S(2)}, u32[]{:S(2)}) collective-permute-start(bf16[448,1024]{1,0:T(8,128)(2,1)S(1)} %add_convert_fusion.3.rest_0_), channel_id=1, source_target_pairs={{2,0},{4,2},{6,4},{8,6},{10,8},{12,10},{14,12},{16,14},{18,16},{20... | collective-permute-start | bytes 2752520 | tf_op jit(solution)/shard_map/ppermute | solution.py:17
  53.5 6.7 %guest_backward.1 = (bf16[448,1024]{1,0:T(8,128)(2,1)S(1)}, f32[448,1024]{1,0:T(8,128)}, bf16[448,384]{1,0:T(8,128)(2,1)S(1)}, bf16[448,384]{1,0:T(8,128)(2,1)S(1)}) custom-call(s32[3]{0:T(128)S(1)} %pad_add_fusion.place, bf16[448,1024]{1,0:T(8,128)(2,1)S(1)} %after.3.cot_m, bf16[448,1024]{1,0:T(8,128)(2,1)S(1)} %constant_dynamic-update-slice_fusion.2.cot_o, ...), custom_call_target="tpu_custom_call" | custom-call | flops 1 | bytes 1 | tf_op jit(solution)/shard_map/guest_backward/pallas_call | solution.py:58
  60.2 0.9 fusion
  61.3 0.5 collective-permute-start.16
  61.8 1.4 %collective-permute-done.17 = bf16[112,1024]{1,0:T(8,128)(2,1)} collective-permute-done((bf16[112,1024]{1,0:T(8,128)(2,1)S(1)}, bf16[112,1024]{1,0:T(8,128)(2,1)}, u32[]{:S(2)}, u32[]{:S(2)}) %collective-permute-start.17) | collective-permute-done | bytes 229408 | tf_op jit(solution)/shard_map/ppermute | solution.py:17
  63.9 1.1 %collective-permute-done.14 = bf16[112,1024]{1,0:T(8,128)(2,1)} collective-permute-done((bf16[112,1024]{1,0:T(8,128)(2,1)}, bf16[112,1024]{1,0:T(8,128)(2,1)}, u32[]{:S(2)}, u32[]{:S(2)}) %collective-permute-start.14) | collective-permute-done | bytes 229408 | tf_op jit(solution)/shard_map/ppermute | solution.py:17
  65.0 2.1 %add_convert_fusion.1.rest_0_ = bf16[448,1024]{1,0:T(8,128)(2,1)S(1)} fusion(f32[448,1024]{1,0:T(8,128)} %get-tuple-element.38, bf16[112,1024]{1,0:T(8,128)(2,1)} %collective-permute-done.17, bf16[112,1024]{1,0:T(8,128)(2,1)} %collective-permute-done.16, bf16[112,1024]{1,0:T(8,128)(2,1)} %collective-permute-done.15, bf16[112,1024]{1,0:T(8,128)(2,1)} %collective-permute-done.14), kind=kLoop, calls=%fused_computation.1 | loop fusion | flops 4587520 | bytes 3670016 | tf_op jit(solution)/shard_map/convert_element_type | solution.py:37
  67.1 1.5 %collective-permute-start.18 = (bf16[448,1024]{1,0:T(8,128)(2,1)S(1)}, bf16[448,1024]{1,0:T(8,128)(2,1)S(1)}, u32[]{:S(2)}, u32[]{:S(2)}) collective-permute-start(bf16[448,1024]{1,0:T(8,128)(2,1)S(1)} %add_convert_fusion.1.rest_0_), channel_id=1, source_target_pairs={{2,0},{4,2},{6,4},{8,6},{10,8},{12,10},{14,12},{16,14},{18,16},{20... | collective-permute-start | bytes 2752520 | tf_op jit(solution)/shard_map/ppermute | solution.py:17
  68.6 6.4 %collective-permute-done.9 = bf16[448,1024]{1,0:T(8,128)(2,1)} collective-permute-done((bf16[448,1024]{1,0:T(8,128)(2,1)S(1)}, bf16[448,1024]{1,0:T(8,128)(2,1)}, u32[]{:S(2)}, u32[]{:S(2)}) %collective-permute-start.9) | collective-permute-done | bytes 917536 | tf_op jit(solution)/shard_map/ppermute | solution.py:17
  75.1 2.9 %add_convert_fusion.2.rest_1_ = bf16[448,1024]{1,0:T(8,128)(2,1)} fusion(bf16[448,1024]{1,0:T(8,128)(2,1)} %collective-permute-done.9, f32[448,1024]{1,0:T(8,128)S(1)} %copy-done.16, bf16[448,1024]{1,0:T(8,128)(2,1)} %collective-permute-done.4, f32[448]{0:T(512)S(1)} %reduce), kind=kLoop, calls=%fused_computation.2 | loop fusion | flops 2752512 | bytes 4589312 | tf_op jit(solution)/shard_map/convert_element_type | solution.py:241
  78.1 7.2 %grads.1 = (bf16[1,2048,384]{2,1,0:T(8,128)(2,1)}, bf16[1,2048,384]{2,1,0:T(8,128)(2,1)}, bf16[1,384,2048]{2,1,0:T(8,128)(2,1)}) custom-call(s32[3]{0:T(128)S(1)} %pad_add_fusion.place, bf16[448,1024]{1,0:T(8,128)(2,1)S(1)} %after.2.tok_m, bf16[448,1024]{1,0:T(8,128)(2,1)S(1)} %copy-done.6, bf16[448,1024]{1,0:T(8,128)(2,1)S(1)} %after.3.cot_m, ...), custom_call_target="tpu_custom_call" | custom-call | flops 99999997952 | bytes 1 | tf_op jit(solution)/shard_map/grads/pallas_call | solution.py:58
  85.3 8.5 %collective-permute-done.18 = bf16[448,1024]{1,0:T(8,128)(2,1)S(1)} collective-permute-done((bf16[448,1024]{1,0:T(8,128)(2,1)S(1)}, bf16[448,1024]{1,0:T(8,128)(2,1)S(1)}, u32[]{:S(2)}, u32[]{:S(2)}) %collective-permute-start.18) | collective-permute-done | bytes 917536 | tf_op jit(solution)/shard_map/ppermute | solution.py:17
  93.8 1.4 %add_convert_fusion = bf16[448,1024]{1,0:T(8,128)(2,1)} fusion(bf16[448,1024]{1,0:T(8,128)(2,1)S(1)} %collective-permute-done.18, f32[448,1024]{1,0:T(8,128)S(1)} %copy-done.14, bf16[448,1024]{1,0:T(8,128)(2,1)S(1)} %collective-permute-done.10), kind=kLoop, calls=%fused_computation | loop fusion | flops 2293760 | bytes 4587520 | tf_op jit(solution)/shard_map/convert_element_type | solution.py:251
  (67 shorter events, 2.0 us)
Async XLA Ops:
  0.6 5.5 %copy-start.1 = (bf16[448,1024]{1,0:T(8,128)(2,1)S(1)}, bf16[448,1024]{1,0:T(8,128)(2,1)}, u32[]{:S(2)}) copy-start(bf16[448,1024]{1,0:T(8,128)(2,1)} %cot_m.1) | copy-start | bytes 2752516
  0.6 7.0 %copy-start.17 = (bf16[14,64]{1,0:T(8,128)(2,1)S(1)}, bf16[14,64]{1,0:T(8,128)(2,1)}, u32[]{:S(2)}) copy-start(bf16[14,64]{1,0:T(8,128)(2,1)} %param.12) | copy-start | bytes 5380
  0.7 7.1 %copy-start.8 = (s32[14]{0:T(128)S(1)}, s32[14]{0:T(128)}, u32[]{:S(2)}) copy-start(s32[14]{0:T(128)} %slot_expert.1) | copy-start | bytes 172
  0.7 7.1 %copy-start.7 = (s32[14,64]{1,0:T(8,128)S(1)}, s32[14,64]{1,0:T(8,128)}, u32[]{:S(2)}) copy-start(s32[14,64]{1,0:T(8,128)} %slot_tokens.1) | copy-start | bytes 10756
  0.7 28.4 %collective-permute-start.5 = (bf16[448,1024]{1,0:T(8,128)(2,1)}, bf16[448,1024]{1,0:T(8,128)(2,1)S(1)}, u32[]{:S(2)}, u32[]{:S(2)}) collective-permute-start(bf16[448,1024]{1,0:T(8,128)(2,1)} %tok_m.1), channel_id=1, source_target_pairs={{30,0},{0,2},{2,4},{4,6},{6,8},{8,10},{10,12},{12,14},{14,16},{16,... | collective-permute-start | bytes 2752520 | tf_op jit(solution)/shard_map/ppermute | solution.py:17
  5.6 3.7 %collective-permute-start.1 = (bf16[224,1024]{1,0:T(8,128)(2,1)S(1)}, bf16[224,1024]{1,0:T(8,128)(2,1)S(1)}, u32[]{:S(2)}, u32[]{:S(2)}) collective-permute-start(bf16[224,1024]{1,0:T(8,128)(2,1)S(1)} %get-tuple-element.60), channel_id=1, source_target_pairs={{1,0},{0,1},{3,2},{2,3},{5,4},{4,5},{7,6},{6,7},{9,8},{8,9},{11,10... | collective-permute-start | bytes 1376264 | tf_op jit(solution)/shard_map/ppermute | solution.py:17
  5.7 5.3 %collective-permute-start = (bf16[224,1024]{1,0:T(8,128)(2,1)}, bf16[224,1024]{1,0:T(8,128)(2,1)}, u32[]{:S(2)}, u32[]{:S(2)}) collective-permute-start(bf16[224,1024]{1,0:T(8,128)(2,1)} %get-tuple-element.59), channel_id=1, source_target_pairs={{1,0},{0,1},{3,2},{2,3},{5,4},{4,5},{7,6},{6,7},{9,8},{8,9},{11,10... | collective-permute-start | bytes 1376264 | tf_op jit(solution)/shard_map/ppermute | solution.py:17
  7.1 4.9 %collective-permute-start.3 = (bf16[224,1024]{1,0:T(8,128)(2,1)}, bf16[224,1024]{1,0:T(8,128)(2,1)}, u32[]{:S(2)}, u32[]{:S(2)}) collective-permute-start(bf16[224,1024]{1,0:T(8,128)(2,1)} %get-tuple-element.58), channel_id=1, source_target_pairs={{1,0},{0,1},{3,2},{2,3},{5,4},{4,5},{7,6},{6,7},{9,8},{8,9},{11,10... | collective-permute-start | bytes 1376264 | tf_op jit(solution)/shard_map/ppermute | solution.py:17
  7.1 4.9 %collective-permute-start.2 = (bf16[224,1024]{1,0:T(8,128)(2,1)}, bf16[224,1024]{1,0:T(8,128)(2,1)}, u32[]{:S(2)}, u32[]{:S(2)}) collective-permute-start(bf16[224,1024]{1,0:T(8,128)(2,1)} %get-tuple-element.57), channel_id=1, source_target_pairs={{1,0},{0,1},{3,2},{2,3},{5,4},{4,5},{7,6},{6,7},{9,8},{8,9},{11,10... | collective-permute-start | bytes 1376264 | tf_op jit(solution)/shard_map/ppermute | solution.py:17
  9.4 3.9 %copy-start.2 = (bf16[448,1024]{1,0:T(8,128)(2,1)S(1)}, bf16[448,1024]{1,0:T(8,128)(2,1)}, u32[]{:S(2)}) copy-start(bf16[448,1024]{1,0:T(8,128)(2,1)} %tok_m.1) | copy-start | bytes 2752516
  9.4 38.5 %collective-permute-start.11 = (bf16[448,1024]{1,0:T(8,128)(2,1)S(1)}, bf16[448,1024]{1,0:T(8,128)(2,1)S(1)}, u32[]{:S(2)}, u32[]{:S(2)}) collective-permute-start(bf16[448,1024]{1,0:T(8,128)(2,1)S(1)} %get-tuple-element.35), channel_id=1, source_target_pairs={{30,0},{0,2},{2,4},{4,6},{6,8},{8,10},{10,12},{12,14},{14,16},{16,... | collective-permute-start | bytes 2752520 | tf_op jit(solution)/shard_map/ppermute | solution.py:17
  25.9 3.2 %copy-start.9 = (bf16[448,1024]{1,0:T(8,128)(2,1)}, bf16[448,1024]{1,0:T(8,128)(2,1)S(1)}, u32[]{:S(2)}) copy-start(bf16[448,1024]{1,0:T(8,128)(2,1)S(1)} %get-tuple-element.34) | copy-start | bytes 2752516
  29.1 1.9 %collective-permute-start.6 = (bf16[224,1024]{1,0:T(8,128)(2,1)S(1)}, bf16[224,1024]{1,0:T(8,128)(2,1)S(1)}, u32[]{:S(2)}, u32[]{:S(2)}) collective-permute-start(bf16[224,1024]{1,0:T(8,128)(2,1)S(1)} %get-tuple-element.56), channel_id=1, source_target_pairs={{1,0},{0,1},{3,2},{2,3},{5,4},{4,5},{7,6},{6,7},{9,8},{8,9},{11,10... | collective-permute-start | bytes 1376264 | tf_op jit(solution)/shard_map/ppermute | solution.py:17
  29.2 2.5 %collective-permute-start.7 = (bf16[224,1024]{1,0:T(8,128)(2,1)S(1)}, bf16[224,1024]{1,0:T(8,128)(2,1)S(1)}, u32[]{:S(2)}, u32[]{:S(2)}) collective-permute-start(bf16[224,1024]{1,0:T(8,128)(2,1)S(1)} %get-tuple-element.55), channel_id=1, source_target_pairs={{1,0},{0,1},{3,2},{2,3},{5,4},{4,5},{7,6},{6,7},{9,8},{8,9},{11,10... | collective-permute-start | bytes 1376264 | tf_op jit(solution)/shard_map/ppermute | solution.py:17
  31.7 6.6 %copy-start.5 = (bf16[448,1024]{1,0:T(8,128)(2,1)}, bf16[448,1024]{1,0:T(8,128)(2,1)S(1)}, u32[]{:S(2)}) copy-start(bf16[448,1024]{1,0:T(8,128)(2,1)S(1)} %constant_dynamic-update-slice_fusion.tok_o) | copy-start | bytes 2752516
  38.3 12.9 %collective-permute-start.8 = (bf16[448,1024]{1,0:T(8,128)(2,1)S(1)}, bf16[448,1024]{1,0:T(8,128)(2,1)S(1)}, u32[]{:S(2)}, u32[]{:S(2)}) collective-permute-start(bf16[448,1024]{1,0:T(8,128)(2,1)S(1)} %get-tuple-element.32.refs_1_), channel_id=1, source_target_pairs={{1,0},{0,1},{3,2},{2,3},{5,4},{4,5},{7,6},{6,7},{9,8},{8,9},{11,10... | collective-permute-start | bytes 2752520 | tf_op jit(solution)/shard_map/ppermute | solution.py:17
  47.9 3.3 %copy-start.15 = (f32[448,1024]{1,0:T(8,128)S(1)}, f32[448,1024]{1,0:T(8,128)}, u32[]{:S(2)}) copy-start(f32[448,1024]{1,0:T(8,128)} %get-tuple-element.31) | copy-start | bytes 5505028
  47.9 1.9 %collective-permute-start.12 = (bf16[224,1024]{1,0:T(8,128)(2,1)S(1)}, bf16[224,1024]{1,0:T(8,128)(2,1)S(1)}, u32[]{:S(2)}, u32[]{:S(2)}) collective-permute-start(bf16[224,1024]{1,0:T(8,128)(2,1)S(1)} %get-tuple-element.54), channel_id=1, source_target_pairs={{1,0},{0,1},{3,2},{2,3},{5,4},{4,5},{7,6},{6,7},{9,8},{8,9},{11,10... | collective-permute-start | bytes 1376264 | tf_op jit(solution)/shard_map/ppermute | solution.py:17
  48.0 3.1 %collective-permute-start.13 = (bf16[224,1024]{1,0:T(8,128)(2,1)S(1)}, bf16[224,1024]{1,0:T(8,128)(2,1)S(1)}, u32[]{:S(2)}, u32[]{:S(2)}) collective-permute-start(bf16[224,1024]{1,0:T(8,128)(2,1)S(1)} %get-tuple-element.53), channel_id=1, source_target_pairs={{1,0},{0,1},{3,2},{2,3},{5,4},{4,5},{7,6},{6,7},{9,8},{8,9},{11,10... | collective-permute-start | bytes 1376264 | tf_op jit(solution)/shard_map/ppermute | solution.py:17
  48.5 20.1 %collective-permute-start.4 = (bf16[448,1024]{1,0:T(8,128)(2,1)}, bf16[448,1024]{1,0:T(8,128)(2,1)}, u32[]{:S(2)}, u32[]{:S(2)}) collective-permute-start(bf16[448,1024]{1,0:T(8,128)(2,1)} %get-tuple-element.29.refs_1_), channel_id=1, source_target_pairs={{1,0},{0,1},{3,2},{2,3},{5,4},{4,5},{7,6},{6,7},{9,8},{8,9},{11,10... | collective-permute-start | bytes 2752520 | tf_op jit(solution)/shard_map/ppermute | solution.py:17
  51.5 23.5 %collective-permute-start.9 = (bf16[448,1024]{1,0:T(8,128)(2,1)S(1)}, bf16[448,1024]{1,0:T(8,128)(2,1)}, u32[]{:S(2)}, u32[]{:S(2)}) collective-permute-start(bf16[448,1024]{1,0:T(8,128)(2,1)S(1)} %add_convert_fusion.3.rest_0_), channel_id=1, source_target_pairs={{2,0},{4,2},{6,4},{8,6},{10,8},{12,10},{14,12},{16,14},{18,16},{20... | collective-permute-start | bytes 2752520 | tf_op jit(solution)/shard_map/ppermute | solution.py:17
  61.3 1.9 %collective-permute-start.17 = (bf16[112,1024]{1,0:T(8,128)(2,1)S(1)}, bf16[112,1024]{1,0:T(8,128)(2,1)}, u32[]{:S(2)}, u32[]{:S(2)}) collective-permute-start(bf16[112,1024]{1,0:T(8,128)(2,1)S(1)} %get-tuple-element.50), channel_id=1, source_target_pairs={{1,0},{0,1},{3,2},{2,3},{5,4},{4,5},{7,6},{6,7},{9,8},{8,9},{11,10... | collective-permute-start | bytes 688136 | tf_op jit(solution)/shard_map/ppermute | solution.py:17
  61.3 2.2 %collective-permute-start.16 = (bf16[112,1024]{1,0:T(8,128)(2,1)}, bf16[112,1024]{1,0:T(8,128)(2,1)}, u32[]{:S(2)}, u32[]{:S(2)}) collective-permute-start(bf16[112,1024]{1,0:T(8,128)(2,1)} %get-tuple-element.51), channel_id=1, source_target_pairs={{1,0},{0,1},{3,2},{2,3},{5,4},{4,5},{7,6},{6,7},{9,8},{8,9},{11,10... | collective-permute-start | bytes 688136 | tf_op jit(solution)/shard_map/ppermute | solution.py:17
  61.8 2.1 %collective-permute-start.15 = (bf16[112,1024]{1,0:T(8,128)(2,1)}, bf16[112,1024]{1,0:T(8,128)(2,1)}, u32[]{:S(2)}, u32[]{:S(2)}) collective-permute-start(bf16[112,1024]{1,0:T(8,128)(2,1)} %get-tuple-element.52), channel_id=1, source_target_pairs={{1,0},{0,1},{3,2},{2,3},{5,4},{4,5},{7,6},{6,7},{9,8},{8,9},{11,10... | collective-permute-start | bytes 688136 | tf_op jit(solution)/shard_map/ppermute | solution.py:17
  63.2 1.8 %collective-permute-start.14 = (bf16[112,1024]{1,0:T(8,128)(2,1)}, bf16[112,1024]{1,0:T(8,128)(2,1)}, u32[]{:S(2)}, u32[]{:S(2)}) collective-permute-start(bf16[112,1024]{1,0:T(8,128)(2,1)} %get-tuple-element.49), channel_id=1, source_target_pairs={{1,0},{0,1},{3,2},{2,3},{5,4},{4,5},{7,6},{6,7},{9,8},{8,9},{11,10... | collective-permute-start | bytes 688136 | tf_op jit(solution)/shard_map/ppermute | solution.py:17
  63.5 21.8 %collective-permute-start.10 = (bf16[448,1024]{1,0:T(8,128)(2,1)}, bf16[448,1024]{1,0:T(8,128)(2,1)S(1)}, u32[]{:S(2)}, u32[]{:S(2)}) collective-permute-start(bf16[448,1024]{1,0:T(8,128)(2,1)} %copy-done.9), channel_id=1, source_target_pairs={{1,0},{0,1},{3,2},{2,3},{5,4},{4,5},{7,6},{6,7},{9,8},{8,9},{11,10... | collective-permute-start | bytes 2752520 | tf_op jit(solution)/shard_map/ppermute | solution.py:17
  65.0 10.1 %copy-start.16 = (f32[448,1024]{1,0:T(8,128)S(1)}, f32[448,1024]{1,0:T(8,128)}, u32[]{:S(2)}) copy-start(f32[448,1024]{1,0:T(8,128)} %get-tuple-element.28) | copy-start | bytes 5505028
  67.1 26.7 %collective-permute-start.18 = (bf16[448,1024]{1,0:T(8,128)(2,1)S(1)}, bf16[448,1024]{1,0:T(8,128)(2,1)S(1)}, u32[]{:S(2)}, u32[]{:S(2)}) collective-permute-start(bf16[448,1024]{1,0:T(8,128)(2,1)S(1)} %add_convert_fusion.1.rest_0_), channel_id=1, source_target_pairs={{2,0},{4,2},{6,4},{8,6},{10,8},{12,10},{14,12},{16,14},{18,16},{20... | collective-permute-start | bytes 2752520 | tf_op jit(solution)/shard_map/ppermute | solution.py:17
  75.1 3.0 %copy-start.4 = (bf16[448,1024]{1,0:T(8,128)(2,1)S(1)}, bf16[448,1024]{1,0:T(8,128)(2,1)}, u32[]{:S(2)}) copy-start(bf16[448,1024]{1,0:T(8,128)(2,1)} %copy-done.3) | copy-start | bytes 2752516
  75.1 3.0 %copy-start.6 = (bf16[448,1024]{1,0:T(8,128)(2,1)S(1)}, bf16[448,1024]{1,0:T(8,128)(2,1)}, u32[]{:S(2)}) copy-start(bf16[448,1024]{1,0:T(8,128)(2,1)} %copy-done.5) | copy-start | bytes 2752516
  75.1 3.0 %copy-start.11 = (bf16[448,384]{1,0:T(8,128)(2,1)S(1)}, bf16[448,384]{1,0:T(8,128)(2,1)}, u32[]{:S(2)}) copy-start(bf16[448,384]{1,0:T(8,128)(2,1)} %copy-done.10) | copy-start | bytes 1032196
  78.1 15.8 %copy-start.14 = (f32[448,1024]{1,0:T(8,128)S(1)}, f32[448,1024]{1,0:T(8,128)}, u32[]{:S(2)}) copy-start(f32[448,1024]{1,0:T(8,128)} %get-tuple-element.33) | copy-start | bytes 5505028
  (5 other events, 10.0 us)
